TPU v7x, 512 devices: a whole 4x4x16 slice. The times are simulated.
512 devices in a mesh: ctx: 64 (over y, z_lo, core), head: 8 (over z_hi, x).
Axes of the slice: x: 4, y: 4, z: 16 (z_hi: 2, z_lo: 8; z = z_hi * 8 + z_lo), core: 2. Of those that a mesh axis runs over, the one named last changes fastest.
Arguments:
- hidden: bfloat16 [4096, 7168], P('ctx', 'head'), may hold values from -6 to 6
- latent_proj: bfloat16 [7168, 576], P('head'), may hold values from -0.0625 to 0.0625
- norm_gain: float32 [512], replicated, may hold values from 0.1 to 1.9
- queries: bfloat16 [4096, 64, 192], P('ctx', 'head'), may hold values from -110 to 110
- key_absorb: bfloat16 [64, 128, 512], P('head'), may hold values from -0.5 to 0.5
- value_absorb: bfloat16 [64, 512, 128], P('head'), may hold values from -0.25 to 0.25
- pool_blocks: bfloat16 [256, 128, 576], P('ctx'), may hold values from -6 to 6
- hit_block: int32 [2], replicated, may hold values from 0 to 255, as said below
Outputs:
- mixed: bfloat16 [4096, 64, 128], P('ctx', 'head')
Inputs may be any that keep to these rules, and one draw needn't show every extreme that they name: `hit_block`: 2 different pool blocks, one of them the pool's last block.
All inputs are finite; a program needn't handle non-finite values.
Results may differ from a plain program's by a relative error of at most 0.017.
The roundings to bfloat16 on the way count: a program that leaves them out, or rounds other values in their place, can miss the bound.
Values may be sent and summed in bfloat16 or wider, within the bound.
No kernel may reach another device: no remote copies, remote signals or barrier semaphores. Data moves between devices by JAX's collectives and lax.ppermute only.
A program may use at most 64 MiB of HBM per device.

v0:
```python
import math

import jax
import jax.numpy as jnp
from jax import lax
from jax.sharding import PartitionSpec as P

EPS = 1e-06
BIG = -1e30


def from_root(block, axis, source):
    block = jnp.where(lax.axis_index(axis) == source, block, jnp.zeros_like(block))
    return lax.psum(block, axis)


def rotate(vector, angle):
    half = vector.shape[-1] // 2
    first = vector[..., :half]
    second = vector[..., half:]
    cosine = jnp.cos(angle)
    sine = jnp.sin(angle)
    return jnp.concatenate(
        [first * cosine - second * sine, second * cosine + first * sine], axis=-1
    )


def angles_for(positions, width):
    half = width // 2
    inverse = 10000.0 ** (-jnp.arange(half, dtype=jnp.float32) / half)
    return positions[:, None] * inverse[None, :]


def finish(raw, positions, norm_gain, rank):
    latent = raw[:, :rank]
    scaled = (
        latent
        * lax.rsqrt(jnp.mean(latent * latent, axis=1, keepdims=True) + EPS)
        * norm_gain[None, :]
    )
    rotated = rotate(raw[:, rank:], angles_for(positions, raw.shape[1] - rank))
    return jnp.concatenate([scaled, rotated], axis=1).astype(jnp.bfloat16)


def attend(carry, query_full, keys, visible, rank, scale):
    peak, total, accum = carry
    scores = jnp.einsum("rc,kc->rk", query_full, keys, preferred_element_type=jnp.float32) * scale
    scores = jnp.where(visible, scores, BIG)
    fresh = jnp.maximum(peak, jnp.max(scores, axis=1))
    weights = jnp.where(visible, jnp.exp(scores - fresh[:, None]), 0.0)
    factor = jnp.exp(peak - fresh)
    total = total * factor + jnp.sum(weights, axis=1)
    accum = accum * factor[:, None] + jnp.dot(
        weights.astype(jnp.bfloat16), keys[:, :rank], preferred_element_type=jnp.float32
    )
    return (fresh, total, accum)


def on_device(
    hidden, latent_proj, norm_gain, queries, key_absorb, value_absorb, pool_blocks, hit_block
):
    tok_rows = queries.shape[0]
    heads_here = queries.shape[1]
    nope = key_absorb.shape[1]
    rank = key_absorb.shape[2]
    width = latent_proj.shape[1]
    block = pool_blocks.shape[1]
    pool_here = pool_blocks.shape[0]
    hit_count = hit_block.shape[0]
    prefix_len = hit_count * block
    scale = 1.0 / math.sqrt(queries.shape[2])
    query_rows = tok_rows * heads_here
    ctx_index = lax.axis_index("ctx")
    first_token = ctx_index * tok_rows
    local_pos = (prefix_len + first_token + jnp.arange(tok_rows)).astype(jnp.float32)
    absorbed = jnp.einsum(
        "thn,hnc->thc", queries[:, :, :nope], key_absorb, preferred_element_type=jnp.float32
    ).astype(jnp.bfloat16)
    rotated_q = rotate(
        queries[:, :, nope:].astype(jnp.float32),
        angles_for(local_pos, queries.shape[2] - nope)[:, None, :],
    ).astype(jnp.bfloat16)
    query_full = jnp.concatenate([absorbed, rotated_q], axis=2).reshape(query_rows, width)
    token_of_row = first_token + jnp.arange(query_rows) // heads_here
    start_state = (
        jnp.full((query_rows,), BIG, jnp.float32),
        jnp.zeros((query_rows,), jnp.float32),
        jnp.zeros((query_rows, rank), jnp.float32),
    )

    def fetch_one(index, carry):
        block_id = hit_block[index]
        owner = block_id // pool_here
        chosen = lax.dynamic_index_in_dim(pool_blocks, block_id % pool_here, 0, keepdims=False)
        arrived = from_root(chosen, "ctx", owner)
        return attend(carry, query_full, arrived, jnp.ones((query_rows, block), bool), rank, scale)

    carry = lax.fori_loop(0, hit_count, fetch_one, start_state)
    partial_raw = jnp.dot(hidden, latent_proj, preferred_element_type=jnp.float32)
    raw = lax.psum(partial_raw, "head")
    new_keys = finish(raw, local_pos, norm_gain, rank)
    piece = lax.all_gather(new_keys, "ctx", axis=0, tiled=True)
    key_index = jnp.arange(piece.shape[0])
    visible = key_index[None, :] <= token_of_row[:, None]
    carry = attend(carry, query_full, piece, visible, rank, scale)
    peak, total, accum = carry
    attended = (accum / total[:, None]).astype(jnp.bfloat16).reshape(tok_rows, heads_here, rank)
    mixed = jnp.einsum("thc,hcv->thv", attended, value_absorb, preferred_element_type=jnp.float32)
    return mixed.astype(jnp.bfloat16)


def solution(mesh):
    placed = (
        P("ctx", "head"),
        P("head", None),
        P(),
        P("ctx", "head", None),
        P("head", None, None),
        P("head", None, None),
        P("ctx", None, None),
        P(),
    )
    return jax.shard_map(
        on_device, mesh=mesh, in_specs=placed, out_specs=P("ctx", "head", None), check_vma=False
    )
```

profile of v0, /device:TPU:1, one launch (start us, length us, event | category | flops | bytes accessed | tf_op | source)
XLA Modules:
  0.0 1850.2 jit_solution(4989391186711577506)
XLA Ops:
  6.5 0.0 copy-start
  6.5 0.0 all-reduce.3.cloned.1.call-start
  6.5 2.5 fusion.43
  9.0 0.0 all-reduce.3.cloned.1.call-update
  9.0 0.0 all-gather.2.cloned.1.call-start
  9.1 149.3 %all-reduce.3.cloned.1.call-done = f32[64,576]{1,0:T(8,128)} async-done(((f32[64,576]{1,0:T(8,128)}), f32[64,576]{1,0:T(8,128)}) %all-reduce.3.cloned.1.call-update) | async-done | bytes 147472 | tf_op jit(solution)/shard_map/psum | solution.py:100
  158.5 1.0 multiply_reduce_fusion
  159.5 1.0 multiply_convert_fusion
  160.5 1.0 multiply_cosine_fusion
  161.5 0.7 pad_maximum_fusion.1
  162.2 0.0 all-gather.2.cloned.1.call-update
  162.3 0.9 slice.37
  163.2 0.9 slice.38
  164.2 0.0 copy-done
  164.2 0.3 fusion.21
  164.5 0.2 subtract_convert_fusion
  164.6 0.1 pad_maximum_fusion
  164.8 0.4 copy.29
  165.1 0.0 copy-start.3
  165.2 118.4 %all-gather.2.cloned.1.call-done = bf16[4096,576]{1,0:T(8,128)(2,1)} async-done(((bf16[64,576]{1,0:T(8,128)(2,1)}), bf16[4096,576]{1,0:T(8,128)(2,1)}) %all-gather.2.cloned.1.call-update) | async-done | bytes 4718608 | tf_op jit(solution)/shard_map/all_gather | solution.py:102
  283.6 9.3 fusion.6
  292.9 0.0 copy-done.3
  292.9 1538.9 %while.20 = (s32[]{:T(128)}, f32[512]{0:T(512)S(1)}, f32[512]{0:T(512)S(1)}, f32[512,512]{1,0:T(8,128)S(1)}, s32[2]{0:T(128)S(1)}, /*index=5*/bf16[4,128,576]{1,...) while((s32[]{:T(128)}, f32[512]{0:T(512)S(1)}, ...), condition=%wide.region_4.5_spmd.clone, body=%wide.region_0.4_spmd.clone.sunk | while | flops 143936032 | bytes 4964832 | solution.py:98
  292.9 0.0 all-reduce.5.cloned.1.call-start
  292.9 0.6 dynamic_slice.27
  296.1 1.6 select_bitcast_fusion.2
  297.7 0.0 all-reduce.5.cloned.1.call-update
  297.7 759.7 %all-reduce.5.cloned.1.call-done = bf16[128,576]{0,1:T(8,128)(2,1)} async-done(((bf16[128,576]{0,1:T(8,128)(2,1)}), bf16[128,576]{0,1:T(8,128)(2,1)}) %all-reduce.5.cloned.1.call-update) | async-done | bytes 147472 | tf_op jit(solution)/shard_map/while/body/eval_jaxpr/psum | solution.py:14
  1057.4 1.3 fusion.62
  1058.7 0.1 fusion.63
  1058.8 1.3 convolution_add_fusion.2
  1060.0 0.0 all-reduce.5.cloned.1.call-start
  1060.1 0.6 dynamic_slice.27
  1063.3 1.6 select_bitcast_fusion.2
  1064.9 0.0 all-reduce.5.cloned.1.call-update
  1064.9 764.2 %all-reduce.5.cloned.1.call-done = bf16[128,576]{0,1:T(8,128)(2,1)} async-done(((bf16[128,576]{0,1:T(8,128)(2,1)}), bf16[128,576]{0,1:T(8,128)(2,1)}) %all-reduce.5.cloned.1.call-update) | async-done | bytes 147472 | tf_op jit(solution)/shard_map/while/body/eval_jaxpr/psum | solution.py:14
  1829.1 1.3 fusion.62
  1830.4 0.1 fusion.63
  1830.5 1.3 convolution_add_fusion.2
  1831.8 0.0 copy-start.1
  1831.8 5.7 fusion.7
  1837.5 0.1 copy-done.1
  1837.6 0.0 copy-start.2
  1837.6 4.9 fusion.27
  1842.6 0.0 copy-done.2
  1842.6 0.4 fusion.22
  1843.0 0.7 copy.17
  (16 shorter events, 0.1 us)
Async XLA Ops:
  6.5 157.6 %copy-start = (bf16[8,128,512]{2,1,0:T(8,128)(2,1)S(1)}, bf16[8,128,512]{2,1,0:T(8,128)(2,1)}, u32[]{:S(2)}) copy-start(bf16[8,128,512]{2,1,0:T(8,128)(2,1)} %param.14) | copy-start | bytes 3145732
  6.5 151.9 %all-reduce.3.cloned.1.call-start = ((), (), s32[]{:S(2)}) async-start(), calls=%async_computation | async-start | bytes 327680 | tf_op jit(solution)/shard_map/psum | solution.py:100
  9.0 274.5 %all-gather.2.cloned.1.call-start = ((), (), s32[]{:S(2)}) async-start(), calls=%async_computation.1 | async-start | bytes 5324800 | tf_op jit(solution)/shard_map/all_gather | solution.py:102
  165.1 127.7 %copy-start.3 = (s32[2]{0:T(128)S(1)}, s32[2]{0:T(128)}, u32[]{:S(2)}) copy-start(s32[2]{0:T(128)} %param.17) | copy-start | bytes 28
  292.9 764.5 %all-reduce.5.cloned.1.call-start = ((), (), s32[]{:S(2)}) async-start(), calls=%async_computation.2 | async-start | bytes 294912 | tf_op jit(solution)/shard_map/while/body/eval_jaxpr/psum | solution.py:14
  1060.0 769.1 %all-reduce.5.cloned.1.call-start = ((), (), s32[]{:S(2)}) async-start(), calls=%async_computation.2 | async-start | bytes 294912 | tf_op jit(solution)/shard_map/while/body/eval_jaxpr/psum | solution.py:14
  1831.8 5.8 copy-start.1
  1837.6 4.9 copy-start.2
Sparse Core Ops, SparseCore 0:
  10.3 148.1 all-reduce.2
  162.4 121.1 all-gather.1
  297.8 759.5 all-reduce.4
  1065.0 764.0 all-reduce.4
where the time goes:
time: 1850 us
  waiting for transfers between devices  1790 us (97%)
  matrix products  22.5 us (1%)
    psum x2, waiting for transfers between devices, from_root(): return lax.psum(block, axis)  1520 us
    psum x1, waiting for transfers between devices, on_device(): raw = lax.psum(partial_raw, 'head')  149 us
    all_gather x1, waiting for transfers between devices, on_device(): piece = lax.all_gather(new_keys, 'ctx', axis=0, tiled=True)  118 us
  transfers between devices with their start and end apart: 4, of which 4 were waited for; matrix products, arithmetic and copies ran while one was open for 0% of the time, Pallas kernels for 0%

commit v1 on v0

v1 whole, which is shorter than its diff:
```python
import functools
import math

import jax
import jax.numpy as jnp
from jax import lax
from jax.experimental import pallas as pl
from jax.experimental.pallas import tpu as pltpu
from jax.sharding import Mesh, PartitionSpec as P

EPS = 1e-06
NEG = -1e30
BF = jnp.bfloat16
F32 = jnp.float32

NY, NZ, NC, NH, NX = 4, 8, 2, 2, 4
CTX = ("y", "zl", "c")
HEAD = ("zh", "x")

TOK = 64
RANK = 512
WIDTH = 576
NOPE = 128
ROPE = 64
QW = 192
HEADS = 8
BLOCK = 128
POOL_HERE = 4
HITS = 2
XROWS = TOK // NX
PREV = 8
PIECE = HITS * PREV
QROWS = TOK * HEADS
PAY = 3 * PIECE
CHUNK = NZ * XROWS + PIECE
NEW = NC * NX * NZ * XROWS
PRE = NX * PIECE
KEYS = NEW + PRE
STAT = 32
OUTR = QROWS + STAT

VMEM = pl.BlockSpec(memory_space=pltpu.VMEM)
SMEM = pl.BlockSpec(memory_space=pltpu.SMEM)


def params(mib=32):
    return pltpu.CompilerParams(vmem_limit_bytes=mib * 2**20)


def swap_halves(v):
    half = v.shape[-1] // 2
    return jnp.concatenate([v[:, half:], v[:, :half]], axis=1)


def prepare_kernel(ids, q_ref, cos_ref, sin_ref, pool_ref, own_q, own_p, p1, p2, p3, qn, qr, pre):
    y, x = ids[0], ids[1]
    flat = q_ref[...].astype(F32).reshape(QROWS, QW)
    qn[...] = flat[:, :NOPE]
    qr[:, :ROPE] = flat[:, NOPE:]
    cosine = cos_ref[...]
    sine = sin_ref[...]
    for h in range(HEADS):
        rope = qr[pl.ds(h, TOK, stride=HEADS), :][:, :ROPE]
        rope = rope * cosine + swap_halves(rope) * sine
        out = jnp.concatenate([qn[pl.ds(h, TOK, stride=HEADS), :], rope], axis=1).astype(BF)
        own_q[h * TOK : (h + 1) * TOK, :] = out
        for p in (p1, p2, p3):
            p[PAY + h * TOK : PAY + (h + 1) * TOK, :] = out
    start = pl.multiple_of(x * 32, 32)
    for b in range(HITS):
        pre[b * 32 : (b + 1) * 32, :] = pool_ref[ids[8 + b], pl.ds(start, 32), :].astype(F32)
    for shift, p in enumerate((own_p, p1, p2, p3)):
        target = lax.rem(y - shift + NY, NY)
        piece = jnp.concatenate(
            [pre[pl.ds(pl.multiple_of(b * 32 + target * PREV, PREV), PREV), :] for b in range(HITS)],
            axis=0,
        )
        for s in range(3):
            p[s * PIECE : (s + 1) * PIECE, :] = piece[:, s * QW : (s + 1) * QW].astype(BF)


def norm_kernel(ids, s_ref, r_ref, gain_ref, cos_ref, sin_ref, own_p, p1, p2, p3, out):
    y, x = ids[0], ids[1]
    raw = s_ref[...] + r_ref[...]
    latent = raw[:, :RANK]
    mean = jnp.mean(latent * latent, axis=1, keepdims=True)
    scaled = latent * lax.rsqrt(mean + EPS) * gain_ref[...]
    start = pl.multiple_of(x * XROWS, XROWS)
    cosine = cos_ref[pl.ds(start, XROWS), :]
    sine = sin_ref[pl.ds(start, XROWS), :]
    rope = raw[:, RANK:]
    rope = rope * cosine + swap_halves(rope) * sine
    keys = jnp.concatenate([scaled, rope], axis=1).astype(BF)
    pieces = []
    row = lax.broadcasted_iota(jnp.int32, (PIECE, QW), 0)
    for s in range(3):
        cand = [p[s * PIECE : (s + 1) * PIECE, :].astype(F32) for p in (own_p, p1, p2, p3)]
        halves = []
        for b in range(HITS):
            shift = lax.rem(ids[2 + b] - y + NY, NY)
            halves.append(
                jnp.where(
                    shift == 0,
                    cand[0],
                    jnp.where(shift == 1, cand[1], jnp.where(shift == 2, cand[2], cand[3])),
                )
            )
        pieces.append(jnp.where(row < PREV, halves[0], halves[1]))
    piece = jnp.concatenate(pieces, axis=1).astype(BF)
    for k in range(NZ):
        out[k, 0:XROWS, :] = keys
        out[k, XROWS : XROWS + PIECE, :] = piece


def pick(first, second):
    row = lax.broadcasted_iota(jnp.int32, (PIECE, WIDTH), 0)
    return jnp.where(row < PREV, first.astype(F32), second.astype(F32)).astype(BF)


def pack_kernel(ids, z_ref, out):
    piece = pick(z_ref[ids[4], XROWS:, :], z_ref[ids[5], XROWS:, :])
    for k in range(NX):
        for z in range(NZ):
            out[k, z * XROWS : (z + 1) * XROWS, :] = z_ref[z, 0:XROWS, :]
        out[k, NZ * XROWS :, :] = piece


def column_to_row(col):
    eye = lax.broadcasted_iota(jnp.int32, (128, 128), 0) == lax.broadcasted_iota(
        jnp.int32, (128, 128), 1
    )
    rows = [
        jnp.sum(jnp.where(eye, col[i * 128 : (i + 1) * 128, :], 0.0), axis=0, keepdims=True)
        for i in range(col.shape[0] // 128)
    ]
    return jnp.concatenate(rows, axis=0)


def row_to_column(rows):
    eye = lax.broadcasted_iota(jnp.int32, (128, 128), 0) == lax.broadcasted_iota(
        jnp.int32, (128, 128), 1
    )
    cols = [
        jnp.sum(jnp.where(eye, rows[i : i + 1, :], 0.0), axis=1, keepdims=True)
        for i in range(rows.shape[0])
    ]
    return jnp.concatenate(cols, axis=0)


def three(v):
    high = v.astype(BF).astype(F32)
    mid = (v - high).astype(BF).astype(F32)
    low = v - high - mid
    return [high, mid, low]


def attend_kernel(ids, q0, q1, q2, q3, here, there, wk, wv, out, keys, qfull, att):
    y = ids[0]
    zl = ids[6]
    c = ids[7]
    scale = 1.0 / math.sqrt(QW)
    for i, ref in enumerate((here, there)):
        for j in range(NX):
            n = (i * NX + j) * NZ * XROWS
            keys[n : n + NZ * XROWS, :] = ref[j, 0 : NZ * XROWS, :]
    for j in range(NX):
        mine = here[j, NZ * XROWS :, :].astype(F32)
        other = there[j, NZ * XROWS :, :].astype(F32)
        keys[NEW + j * PIECE : NEW + (j + 1) * PIECE, :] = pick(
            jnp.where(ids[10] == c, mine, other), jnp.where(ids[11] == c, mine, other)
        )
    sources = (q0, q1, q2, q3)
    starts = (0, PAY, PAY, PAY)
    for h in range(HEADS):
        rows = jnp.concatenate(
            [q[s + h * TOK : s + (h + 1) * TOK, :] for q, s in zip(sources, starts)], axis=0
        )
        absorbed = jnp.dot(rows[:, :NOPE], wk[h], preferred_element_type=F32).astype(BF)
        full = jnp.concatenate([absorbed, rows[:, NOPE:]], axis=1)
        for g in range(NY):
            qfull[g, h * TOK : (h + 1) * TOK, :] = full[g * TOK : (g + 1) * TOK, :]

    col = lax.broadcasted_iota(jnp.int32, (1, KEYS), 1)
    zz = lax.rem(lax.div(col, XROWS), NZ)
    xx = lax.rem(lax.div(col, XROWS * NZ), NX)
    cc = lax.div(col, XROWS * NZ * NX)
    cc = jnp.where(cc == 0, c, 1 - c)
    token = zz * (NC * TOK) + cc * TOK + xx * XROWS + lax.rem(col, XROWS) + y * (NZ * NC * TOK)
    token = jnp.where(col < NEW, token, -1)
    for g in range(NY):
        yq = lax.rem(y + g, NY)
        scores = lax.dot_general(
            qfull[g], keys[...], (((1,), (1,)), ((), ())), preferred_element_type=F32
        )
        mine = lax.rem(lax.broadcasted_iota(jnp.int32, (QROWS, 1), 0), TOK)
        mine = mine + (yq * NZ * NC + zl * NC + c) * TOK
        visible = token <= mine
        scores = jnp.where(visible, scores, NEG)
        peak = jnp.max(scores, axis=1, keepdims=True)
        weights = jnp.exp((scores - peak) * scale)
        total = jnp.sum(weights, axis=1, keepdims=True)
        accum = jnp.dot(weights.astype(BF), keys[:, :RANK], preferred_element_type=F32)
        partial = (accum / total).astype(BF)
        for h in range(HEADS):
            att[h, g * TOK : (g + 1) * TOK, :] = partial[h * TOK : (h + 1) * TOK, :]
        stats = [column_to_row(v) for v in three(peak * scale) + three(total)]
        stats.append(jnp.zeros((STAT - 4 * len(stats), 128), F32))
        out[yq, QROWS:, :] = jnp.concatenate(stats, axis=0).astype(BF)
    for h in range(HEADS):
        mixed = jnp.dot(att[h], wv[h], preferred_element_type=F32).astype(BF)
        for g in range(NY):
            yq = lax.rem(y + g, NY)
            out[yq, h * TOK : (h + 1) * TOK, :] = mixed[g * TOK : (g + 1) * TOK, :]


def merge_kernel(p_ref, out, flat):
    peaks, totals = [], []
    for s in range(NY):
        stats = p_ref[s, QROWS:, :].astype(F32)
        peaks.append(row_to_column(stats[0:4] + stats[4:8] + stats[8:12]))
        totals.append(row_to_column(stats[12:16] + stats[16:20] + stats[20:24]))
    peak = functools.reduce(jnp.maximum, peaks)
    weights = [t * jnp.exp(p - peak) for t, p in zip(totals, peaks)]
    total = functools.reduce(jnp.add, weights)
    mixed = sum(p_ref[s, 0:QROWS, :].astype(F32) * (weights[s] / total) for s in range(NY))
    for h in range(HEADS):
        flat[pl.ds(h, TOK, stride=HEADS), :] = mixed[h * TOK : (h + 1) * TOK, :]
    out[...] = flat[...].reshape(TOK, HEADS, 128).astype(BF)


def on_device(
    hidden, latent_proj, norm_gain, queries, key_absorb, value_absorb, pool_blocks, hit_block
):
    y, zl, c, x = (lax.axis_index(a) for a in ("y", "zl", "c", "x"))
    owner = hit_block // POOL_HERE
    ids = jnp.concatenate(
        [
            jnp.stack([y, x]),
            owner // (NZ * NC),
            (owner // NC) % NZ,
            jnp.stack([zl, c]),
            hit_block % POOL_HERE,
            owner % NC,
        ]
    ).astype(jnp.int32)
    first = HITS * BLOCK + ((y * NZ + zl) * NC + c) * TOK
    positions = (first + jnp.arange(TOK)).astype(F32)
    half = ROPE // 2
    inverse = 10000.0 ** (-jnp.arange(half, dtype=F32) / half)
    angle = positions[:, None] * inverse[None, :]
    cosine, sine = jnp.cos(angle), jnp.sin(angle)
    cosine = jnp.concatenate([cosine, cosine], axis=1)
    sine = jnp.concatenate([-sine, sine], axis=1)

    pay = jax.ShapeDtypeStruct((PAY + QROWS, QW), BF)
    own_q, own_p, p1, p2, p3 = pl.pallas_call(
        prepare_kernel,
        out_shape=[
            jax.ShapeDtypeStruct((QROWS, QW), BF),
            jax.ShapeDtypeStruct((PAY, QW), BF),
            pay,
            pay,
            pay,
        ],
        in_specs=[SMEM] + [VMEM] * 4,
        out_specs=[VMEM] * 5,
        scratch_shapes=[
            pltpu.VMEM((QROWS, 128), F32),
            pltpu.VMEM((QROWS, 128), F32),
            pltpu.VMEM((HITS * 32, WIDTH), F32),
        ],
        compiler_params=params(),
        name="prepare",
    )(ids, queries, cosine, sine, pool_blocks)
    received = [
        lax.ppermute(p, "y", [(i, (i - k) % NY) for i in range(NY)])
        for k, p in zip((1, 2, 3), (p1, p2, p3))
    ]

    partial_raw = jnp.dot(hidden, latent_proj, preferred_element_type=F32)
    parts = lax.all_to_all(partial_raw.reshape(NX, XROWS, WIDTH), "x", 0, 0)
    mine = jnp.sum(parts, axis=0)
    other = lax.ppermute(mine, "zh", [(0, 1), (1, 0)])
    head = pl.BlockSpec((PAY, QW), lambda i: (0, 0))

    def whole(shape):
        return pl.BlockSpec(shape, lambda i: (0,) * len(shape))

    packed = pl.pallas_call(
        norm_kernel,
        grid=(1,),
        out_shape=jax.ShapeDtypeStruct((NZ, XROWS + PIECE, WIDTH), BF),
        in_specs=[
            SMEM,
            whole((XROWS, WIDTH)),
            whole((XROWS, WIDTH)),
            whole((1, RANK)),
            whole((TOK, ROPE)),
            whole((TOK, ROPE)),
            head,
            head,
            head,
            head,
        ],
        out_specs=whole((NZ, XROWS + PIECE, WIDTH)),
        compiler_params=params(),
        name="norm",
    )(ids, mine, other, norm_gain[None, :], cosine, sine, own_p, *received)
    along_z = lax.all_to_all(packed, "zl", 0, 0)
    packed = pl.pallas_call(
        pack_kernel,
        out_shape=jax.ShapeDtypeStruct((NX, CHUNK, WIDTH), BF),
        in_specs=[SMEM, VMEM],
        out_specs=VMEM,
        compiler_params=params(),
        name="pack",
    )(ids, along_z)
    along_x = lax.all_to_all(packed, "x", 0, 0)
    from_core = lax.ppermute(along_x, "c", [(0, 1), (1, 0)])
    out = pl.pallas_call(
        attend_kernel,
        out_shape=jax.ShapeDtypeStruct((NY, OUTR, 128), BF),
        in_specs=[SMEM] + [VMEM] * 8,
        out_specs=VMEM,
        scratch_shapes=[
            pltpu.VMEM((KEYS, WIDTH), BF),
            pltpu.VMEM((NY, QROWS, WIDTH), BF),
            pltpu.VMEM((HEADS, NY * TOK, RANK), BF),
        ],
        compiler_params=params(48),
        name="attend",
    )(ids, own_q, *received, along_x, from_core, key_absorb, value_absorb)
    back = lax.all_to_all(out, "y", 0, 0)
    return pl.pallas_call(
        merge_kernel,
        out_shape=jax.ShapeDtypeStruct((TOK, HEADS, 128), BF),
        in_specs=[VMEM],
        out_specs=VMEM,
        scratch_shapes=[pltpu.VMEM((QROWS, 128), F32)],
        compiler_params=params(),
        name="merge",
    )(back)


def solution(mesh):
    fine = Mesh(mesh.devices.reshape(NY, NZ, NC, NH, NX), CTX + HEAD)
    placed = (
        P(CTX, HEAD),
        P(HEAD, None),
        P(),
        P(CTX, HEAD, None),
        P(HEAD, None, None),
        P(HEAD, None, None),
        P(CTX, None, None),
        P(),
    )
    return jax.shard_map(
        on_device, mesh=fine, in_specs=placed, out_specs=P(CTX, HEAD, None), check_vma=False
    )
```

time: 1850 us -> 113 us (0.06)
  waiting for transfers between devices: 1790 us -> 3.2 us
  blocking collectives: 0 us -> 54.4 us
  starting transfers between devices: 0.09 us -> 36.4 us
  matrix products: 22.5 us -> 0.44 us
    psum x3 -> x0, waiting for transfers between devices: 1670 us -> none  [the longest x2 1520 us: from_root(): return lax.psum(block, axis)]
    all_gather x1 -> x0, waiting for transfers between devices: 118 us -> none  [on_device(): piece = lax.all_gather(new_keys, 'ctx', axis=0, tiled=True)]
    all_to_all x0 -> x4, blocking collectives: none -> 54.4 us  [the longest x1 22.4 us: on_device(): along_z = lax.all_to_all(packed, 'zl', 0, 0)]
    ppermute x0 -> x5, starting transfers between devices: none -> 36.4 us  [the longest x1 15.2 us: on_device(): other = lax.ppermute(mine, 'zh', [(0, 1), (1, 0)])]
    dot_general x9 -> x1, matrix products: 22.5 us -> 0.44 us  [on_device(): partial_raw = jnp.dot(hidden, latent_proj, preferred_element_type=F32)]
  transfers between devices with their start and end apart: 4 -> 5, of which waited for: 4 -> 2; matrix products, arithmetic and copies ran while one was open for 0% -> 0% of each run, Pallas kernels for 0% -> 0%
where the time goes in v1:
time: 113 us; the launch traced here: 112 us
  blocking collectives  54.4 us (48%)
  starting transfers between devices  36.4 us (32%)
  Pallas kernels  14.5 us (13%)
  waiting for transfers between devices  3.2 us (3%)
  local copies, waits for them, and re-layouts  2.75 us (2%)
    all_to_all x1, blocking collectives, on_device(): along_z = lax.all_to_all(packed, 'zl', 0, 0)  22.4 us
    ppermute x1, starting transfers between devices, on_device(): other = lax.ppermute(mine, 'zh', [(0, 1), (1, 0)])  15.2 us
    all_to_all x1, blocking collectives, on_device(): back = lax.all_to_all(out, 'y', 0, 0)  12.2 us
    ppermute x1, starting transfers between devices, on_device(): from_core = lax.ppermute(along_x, 'c', [(0, 1), (1, 0)])  10.9 us
    pallas_call x1, Pallas kernels, on_device(): pl.pallas_call(attend_kernel, out_shape=jax.ShapeDtypeStruct((NY, OUTR, 1...  10.8 us
    all_to_all x1, blocking collectives, on_device(): along_x = lax.all_to_all(packed, 'x', 0, 0)  10.6 us
    ppermute x3, starting transfers between devices, on_device(): lax.ppermute(p, 'y', [(i, (i - k) % NY) for i in range(NY)])  10.3 us
    all_to_all x1, blocking collectives, on_device(): parts = lax.all_to_all(partial_raw.reshape(NX, XROWS, WIDTH), 'x', 0, 0)  9.11 us
  transfers between devices with their start and end apart: 5, of which 2 were waited for; matrix products, arithmetic and copies ran while one was open for 0% of the time, Pallas kernels for 0%

profile of v1, /device:TPU:1, one launch (start us, length us, event | category | flops | bytes accessed | tf_op | source)
XLA Modules:
  0.0 112.2 jit_solution(15995595241266656077)
XLA Ops:
  0.0 0.0 copy-start
  0.0 0.0 copy-start.6
  0.0 0.7 copy-done.6
  0.8 1.4 %copy.9.pool_ref = bf16[4,128,576]{2,1,0:T(8,128)(2,1)S(1)} copy(bf16[4,128,576]{1,2,0:T(8,128)(2,1)} %param.14) | data formatting | bytes 1179648 | tf_op args[6]
  2.2 0.0 copy-start.3
  2.2 0.2 fusion
  2.4 0.1 pad_maximum_fusion
  2.5 0.1 concatenate.9.ids
  2.6 0.6 copy-done.3
  3.1 0.0 copy-start.5
  3.1 0.8 prepare.1
  3.9 5.5 %collective-permute-start = (bf16[560,192]{1,0:T(8,128)(2,1)S(1)}, bf16[560,192]{1,0:T(8,128)(2,1)S(1)}, u32[]{:S(2)}, u32[]{:S(2)}) collective-permute-start(bf16[560,192]{1,0:T(8,128)(2,1)S(1)} %get-tuple-element.11), channel_id=1, source_target_pairs={{0,384},{128,0},{256,128},{384,256},{1,385},{129,1},{257,129},{385... | collective-permute-start | bytes 645128 | tf_op jit(solution)/shard_map/ppermute | solution.py:276
  9.4 2.3 %collective-permute-start.1 = (bf16[560,192]{1,0:T(8,128)(2,1)S(1)}, bf16[560,192]{1,0:T(8,128)(2,1)S(1)}, u32[]{:S(2)}, u32[]{:S(2)}) collective-permute-start(bf16[560,192]{1,0:T(8,128)(2,1)S(1)} %get-tuple-element.12), channel_id=1, source_target_pairs={{0,256},{128,384},{256,0},{384,128},{1,257},{129,385},{257,1},{385... | collective-permute-start | bytes 645128 | tf_op jit(solution)/shard_map/ppermute | solution.py:276
  11.7 2.6 %collective-permute-start.2 = (bf16[560,192]{1,0:T(8,128)(2,1)S(1)}, bf16[560,192]{1,0:T(8,128)(2,1)S(1)}, u32[]{:S(2)}, u32[]{:S(2)}) collective-permute-start(bf16[560,192]{1,0:T(8,128)(2,1)S(1)} %get-tuple-element.13), channel_id=1, source_target_pairs={{0,128},{128,256},{256,384},{384,0},{1,129},{129,257},{257,385},{3... | collective-permute-start | bytes 645128 | tf_op jit(solution)/shard_map/ppermute | solution.py:276
  14.3 0.0 copy-done
  14.3 0.0 copy-done.5
  14.3 0.4 fusion.2
  14.8 9.1 %all_to_all.20 = f32[4,16,576]{2,1,0:T(8,128)S(1)} all-to-all(f32[4,16,576]{2,1,0:T(8,128)S(1)} %bitcast.9), channel_id=1, replica_groups=mesh['y'=4,'zl'=8,'c'=2,'zh'=2,'x'=4] {'x'}, dimensions={0} | all-to-all | bytes 294912 | tf_op jit(solution)/shard_map/all_to_all | solution.py:281
  23.9 0.0 copy-start.4
  23.9 15.2 %collective-permute-start.3 = (f32[16,576]{1,0:T(8,128)S(1)}, f32[16,576]{1,0:T(8,128)S(1)}, u32[]{:S(2)}, u32[]{:S(2)}) collective-permute-start(f32[16,576]{1,0:T(8,128)S(1)} %reduce_sum.9.s_ref), channel_id=1, source_target_pairs={{0,4},{4,0},{1,5},{5,1},{2,6},{6,2},{3,7},{7,3},{8,12},{12,8},{9,1... | collective-permute-start | bytes 110600 | tf_op jit(solution)/shard_map/ppermute | solution.py:283
  39.1 1.4 %collective-permute-done.3.r_ref = f32[16,576]{1,0:T(8,128)S(1)} collective-permute-done((f32[16,576]{1,0:T(8,128)S(1)}, f32[16,576]{1,0:T(8,128)S(1)}, u32[]{:S(2)}, u32[]{:S(2)}) %collective-permute-start.3) | collective-permute-done | bytes 36896 | tf_op jit(solution)/shard_map/ppermute | solution.py:283
  40.4 0.0 collective-permute-done.p1.q1
  40.4 0.0 collective-permute-done.1.p2.q2
  40.5 0.0 collective-permute-done.2.p3.q3
  40.5 0.0 copy-done.4
  40.5 0.6 norm.1
  41.1 22.4 %all_to_all.21.z_ref = bf16[8,32,576]{2,1,0:T(8,128)(2,1)S(1)} all-to-all(bf16[8,32,576]{2,1,0:T(8,128)(2,1)S(1)} %norm.1), channel_id=1, replica_groups=mesh['y'=4,'zl'=8,'c'=2,'zh'=2,'x'=4] {'zl'}, dimensions={0} | all-to-all | bytes 589824 | tf_op jit(solution)/shard_map/all_to_all | solution.py:309
  63.6 0.0 copy-start.1
  63.6 0.0 copy-start.2
  63.6 0.6 pack.1
  64.2 10.6 %all_to_all.22.here = bf16[4,144,576]{2,1,0:T(8,128)(2,1)S(1)} all-to-all(bf16[4,144,576]{2,1,0:T(8,128)(2,1)S(1)} %pack.1), channel_id=1, replica_groups=mesh['y'=4,'zl'=8,'c'=2,'zh'=2,'x'=4] {'x'}, dimensions={0} | all-to-all | bytes 1327104 | tf_op jit(solution)/shard_map/all_to_all | solution.py:318
  74.8 10.9 %collective-permute-start.4 = (bf16[4,144,576]{2,1,0:T(8,128)(2,1)S(1)}, bf16[4,144,576]{2,1,0:T(8,128)(2,1)S(1)}, u32[]{:S(2)}, u32[]{:S(2)}) collective-permute-start(bf16[4,144,576]{2,1,0:T(8,128)(2,1)S(1)} %all_to_all.22.here), channel_id=1, source_target_pairs={{0,8},{8,0},{1,9},{9,1},{2,10},{10,2},{3,11},{11,3},{4,12},{12,4},... | collective-permute-start | bytes 1990664 | tf_op jit(solution)/shard_map/ppermute | solution.py:319
  85.7 1.8 %collective-permute-done.4.there = bf16[4,144,576]{2,1,0:T(8,128)(2,1)S(1)} collective-permute-done((bf16[4,144,576]{2,1,0:T(8,128)(2,1)S(1)}, bf16[4,144,576]{2,1,0:T(8,128)(2,1)S(1)}, u32[]{:S(2)}, u32[]{:S(2)}) %collective-permute-start.4) | collective-permute-done | bytes 663584 | tf_op jit(solution)/shard_map/ppermute | solution.py:319
  87.5 0.0 copy-done.1
  87.5 0.0 copy-done.2
  87.5 10.8 %attend.1 = bf16[4,544,128]{2,1,0:T(8,128)(2,1)S(1)} custom-call(s32[12]{0:T(128)S(1)} %concatenate.9.ids, bf16[512,192]{1,0:T(8,128)(2,1)S(1)} %get-tuple-element.10.q0, bf16[560,192]{1,0:T(8,128)(2,1)S(1)} %collective-permute-done.p1.q1, bf16[560,192]{1,0:T(8,128)(2,1)S(1)} %collective-permute-done.1.p2.q2, ...), custom_call_target="tpu_custom_call" | custom-call | tf_op jit(solution)/shard_map/attend/pallas_call | solution.py:320
  98.3 12.2 %all_to_all.23.p_ref = bf16[4,544,128]{2,1,0:T(8,128)(2,1)S(1)} all-to-all(bf16[4,544,128]{2,1,0:T(8,128)(2,1)S(1)} %attend.1), channel_id=1, replica_groups=mesh['y'=4,'zl'=8,'c'=2,'zh'=2,'x'=4] {'y'}, dimensions={0} | all-to-all | bytes 1114112 | tf_op jit(solution)/shard_map/all_to_all | solution.py:333
  110.5 1.7 %merge.1 = bf16[64,8,128]{2,1,0:T(8,128)(2,1)} custom-call(bf16[4,544,128]{2,1,0:T(8,128)(2,1)S(1)} %all_to_all.23.p_ref), custom_call_target="tpu_custom_call" | custom-call | tf_op jit(solution)/shard_map/merge/pallas_call | solution.py:334
  (5 shorter events, 0.1 us)
Async XLA Ops:
  0.0 14.3 %copy-start = (bf16[896,576]{0,1:T(8,128)(2,1)S(1)}, bf16[896,576]{0,1:T(8,128)(2,1)}, u32[]{:S(2)}) copy-start(bf16[896,576]{0,1:T(8,128)(2,1)} %param.9) | copy-start | bytes 3096580
  0.0 0.7 copy-start.6
  2.2 1.0 copy-start.3
  3.1 11.2 %copy-start.5 = (bf16[64,896]{1,0:T(8,128)(2,1)S(1)}, bf16[64,896]{1,0:T(8,128)(2,1)}, u32[]{:S(2)}) copy-start(bf16[64,896]{1,0:T(8,128)(2,1)} %param.8) | copy-start | bytes 344068
  3.9 36.5 %collective-permute-start = (bf16[560,192]{1,0:T(8,128)(2,1)S(1)}, bf16[560,192]{1,0:T(8,128)(2,1)S(1)}, u32[]{:S(2)}, u32[]{:S(2)}) collective-permute-start(bf16[560,192]{1,0:T(8,128)(2,1)S(1)} %get-tuple-element.11), channel_id=1, source_target_pairs={{0,384},{128,0},{256,128},{384,256},{1,385},{129,1},{257,129},{385... | collective-permute-start | bytes 645128 | tf_op jit(solution)/shard_map/ppermute | solution.py:276
  9.4 31.0 %collective-permute-start.1 = (bf16[560,192]{1,0:T(8,128)(2,1)S(1)}, bf16[560,192]{1,0:T(8,128)(2,1)S(1)}, u32[]{:S(2)}, u32[]{:S(2)}) collective-permute-start(bf16[560,192]{1,0:T(8,128)(2,1)S(1)} %get-tuple-element.12), channel_id=1, source_target_pairs={{0,256},{128,384},{256,0},{384,128},{1,257},{129,385},{257,1},{385... | collective-permute-start | bytes 645128 | tf_op jit(solution)/shard_map/ppermute | solution.py:276
  11.7 28.8 %collective-permute-start.2 = (bf16[560,192]{1,0:T(8,128)(2,1)S(1)}, bf16[560,192]{1,0:T(8,128)(2,1)S(1)}, u32[]{:S(2)}, u32[]{:S(2)}) collective-permute-start(bf16[560,192]{1,0:T(8,128)(2,1)S(1)} %get-tuple-element.13), channel_id=1, source_target_pairs={{0,128},{128,256},{256,384},{384,0},{1,129},{129,257},{257,385},{3... | collective-permute-start | bytes 645128 | tf_op jit(solution)/shard_map/ppermute | solution.py:276
  23.9 16.6 %copy-start.4 = (f32[512]{0:T(512)S(1)}, f32[512]{0:T(512)}, u32[]{:S(2)}) copy-start(f32[512]{0:T(512)} %param.10) | copy-start | bytes 6148
  23.9 16.5 %collective-permute-start.3 = (f32[16,576]{1,0:T(8,128)S(1)}, f32[16,576]{1,0:T(8,128)S(1)}, u32[]{:S(2)}, u32[]{:S(2)}) collective-permute-start(f32[16,576]{1,0:T(8,128)S(1)} %reduce_sum.9.s_ref), channel_id=1, source_target_pairs={{0,4},{4,0},{1,5},{5,1},{2,6},{6,2},{3,7},{7,3},{8,12},{12,8},{9,1... | collective-permute-start | bytes 110600 | tf_op jit(solution)/shard_map/ppermute | solution.py:283
  63.6 24.0 %copy-start.1 = (bf16[8,128,512]{2,1,0:T(8,128)(2,1)S(1)}, bf16[8,128,512]{2,1,0:T(8,128)(2,1)}, u32[]{:S(2)}) copy-start(bf16[8,128,512]{2,1,0:T(8,128)(2,1)} %wk.1) | copy-start | bytes 3145732
  63.6 24.0 %copy-start.2 = (bf16[8,512,128]{2,1,0:T(8,128)(2,1)S(1)}, bf16[8,512,128]{2,1,0:T(8,128)(2,1)}, u32[]{:S(2)}) copy-start(bf16[8,512,128]{2,1,0:T(8,128)(2,1)} %wv.1) | copy-start | bytes 3145732
  74.8 12.8 %collective-permute-start.4 = (bf16[4,144,576]{2,1,0:T(8,128)(2,1)S(1)}, bf16[4,144,576]{2,1,0:T(8,128)(2,1)S(1)}, u32[]{:S(2)}, u32[]{:S(2)}) collective-permute-start(bf16[4,144,576]{2,1,0:T(8,128)(2,1)S(1)} %all_to_all.22.here), channel_id=1, source_target_pairs={{0,8},{8,0},{1,9},{9,1},{2,10},{10,2},{3,11},{11,3},{4,12},{12,4},... | collective-permute-start | bytes 1990664 | tf_op jit(solution)/shard_map/ppermute | solution.py:319

commit v2 on v1

v2 whole, which is shorter than its diff:
```python
import functools
import math

import jax
import jax.numpy as jnp
from jax import lax
from jax.experimental import pallas as pl
from jax.experimental.pallas import tpu as pltpu
from jax.sharding import Mesh, PartitionSpec as P

EPS = 1e-06
NEG = -1e30
BF = jnp.bfloat16
F32 = jnp.float32

NY, NZ, NC, NH, NX = 4, 8, 2, 2, 4
CTX = ("y", "zl", "c")
HEAD = ("zh", "x")

TOK = 64
RANK = 512
WIDTH = 576
NOPE = 128
ROPE = 64
QW = 192
HEADS = 8
BLOCK = 128
POOL_HERE = 4
HITS = 2
XROWS = TOK // NX
PREV = 8
PIECE = HITS * PREV
QROWS = TOK * HEADS
LANES = 128
BANDS = RANK // LANES
PAY = (BANDS + 1) * PIECE
PAYQ = PAY + QROWS
PAYR = PAYQ + QROWS // 2
RAWR = BANDS * XROWS + XROWS // 2
ZBAND = XROWS + PIECE
ZROWS = BANDS * ZBAND + 16
SPAN = NZ * XROWS
XBAND = SPAN + PIECE
XROPE = BANDS * XBAND
XPRE = XROPE + SPAN // 2
CHUNK = XPRE + PIECE
NEW = NC * NX * NZ * XROWS
PRE = NX * PIECE
KEYS = NEW + PRE
STAT = 32
OUTR = QROWS + STAT
ROWS = 512

VMEM = pl.BlockSpec(memory_space=pltpu.VMEM)
SMEM = pl.BlockSpec(memory_space=pltpu.SMEM)


def params(mib=32):
    return pltpu.CompilerParams(vmem_limit_bytes=mib * 2**20)


def swap_halves(v):
    half = v.shape[-1] // 2
    return jnp.concatenate([v[:, half:], v[:, :half]], axis=1)


def prepare_kernel(
    hit, q_ref, cos_ref, sin_ref, pool_ref, own_q, own_p, p1, p2, p3, qn, qr, found, pre, sem
):
    y, x = lax.axis_index("y"), lax.axis_index("x")
    copies = [
        pltpu.make_async_copy(pool_ref.at[lax.rem(hit[b], POOL_HERE)], found.at[b], sem.at[b])
        for b in range(HITS)
    ]
    for copy in copies:
        copy.start()
    flat = q_ref[...].astype(F32).reshape(QROWS, QW)
    qn[...] = flat[:, :NOPE]
    qr[:, :ROPE] = flat[:, NOPE:]
    cosine = cos_ref[...]
    sine = sin_ref[...]
    ropes = []
    for h in range(HEADS):
        rope = qr[pl.ds(h, TOK, stride=HEADS), :][:, :ROPE]
        ropes.append(rope * cosine + swap_halves(rope) * sine)
        out = qn[pl.ds(h, TOK, stride=HEADS), :].astype(BF)
        own_q[h * TOK : (h + 1) * TOK, :] = out
        for p in (p1, p2, p3):
            p[PAY + h * TOK : PAY + (h + 1) * TOK, :] = out
    for h in range(HEADS // 2):
        out = jnp.concatenate([ropes[h], ropes[h + HEADS // 2]], axis=1).astype(BF)
        own_q[QROWS + h * TOK : QROWS + (h + 1) * TOK, :] = out
        for p in (p1, p2, p3):
            p[PAYQ + h * TOK : PAYQ + (h + 1) * TOK, :] = out
    for b in range(HITS):
        copies[b].wait()
        pre[b * BLOCK : (b + 1) * BLOCK, :] = found[b].astype(F32).T
    for shift, p in enumerate((own_p, p1, p2, p3)):
        target = lax.rem(y - shift + NY, NY)
        first = x * (BLOCK // NX) + target * PREV
        piece = jnp.concatenate(
            [pre[pl.ds(pl.multiple_of(b * BLOCK + first, PREV), PREV), :] for b in range(HITS)],
            axis=0,
        )
        piece = jnp.concatenate([piece, piece[:, RANK:]], axis=1).astype(BF)
        for s in range(BANDS + 1):
            p[s * PIECE : (s + 1) * PIECE, :] = piece[:, s * LANES : (s + 1) * LANES]


def project_kernel(hidden, proj, out):
    partial = lax.dot_general(
        hidden[...], proj[...], (((1,), (1,)), ((), ())), preferred_element_type=F32
    )
    for k in range(NX):
        rows = partial[k * XROWS : (k + 1) * XROWS]
        for s in range(BANDS):
            out[k, s * XROWS : (s + 1) * XROWS, :] = rows[:, s * LANES : (s + 1) * LANES]
        rope = rows[:, RANK:]
        half = XROWS // 2
        out[k, BANDS * XROWS :, :] = jnp.concatenate([rope[:half], rope[half:]], axis=1)


def norm_kernel(ids, s_ref, r_ref, gain_ref, cos_ref, sin_ref, own_p, p1, p2, p3, out):
    y, x = ids[0], ids[1]
    raw = s_ref[...] + r_ref[...]
    latent = jnp.concatenate([raw[s * XROWS : (s + 1) * XROWS] for s in range(BANDS)], axis=1)
    rope = raw[BANDS * XROWS :]
    rope = jnp.concatenate([rope[:, :ROPE], rope[:, ROPE:]], axis=0)
    mean = jnp.mean(latent * latent, axis=1, keepdims=True)
    scaled = (latent * lax.rsqrt(mean + EPS) * gain_ref[...]).astype(BF)
    start = pl.multiple_of(x * XROWS, XROWS)
    cosine = cos_ref[pl.ds(start, XROWS), :]
    sine = sin_ref[pl.ds(start, XROWS), :]
    rope = rope * cosine + swap_halves(rope) * sine
    shifts = [lax.rem(ids[2 + b] - y + NY, NY) for b in range(HITS)]
    row = lax.broadcasted_iota(jnp.int32, (PIECE, LANES), 0)
    bands = []
    for s in range(BANDS + 1):
        cand = [p[s * PIECE : (s + 1) * PIECE, :].astype(F32) for p in (own_p, p1, p2, p3)]
        halves = [
            jnp.where(
                shift == 0,
                cand[0],
                jnp.where(shift == 1, cand[1], jnp.where(shift == 2, cand[2], cand[3])),
            )
            for shift in shifts
        ]
        bands.append(jnp.where(row < PREV, halves[0], halves[1]))
    ropes = jnp.concatenate([rope, bands[BANDS][:, :ROPE]], axis=1).astype(BF)
    for k in range(NZ):
        for s in range(BANDS):
            n = s * ZBAND
            out[k, n : n + XROWS, :] = scaled[:, s * LANES : (s + 1) * LANES]
            out[k, n + XROWS : n + ZBAND, :] = bands[s].astype(BF)
        out[k, BANDS * ZBAND :, :] = ropes


def pick(first, second):
    row = lax.broadcasted_iota(jnp.int32, (PIECE, LANES), 0)
    return jnp.where(row < PREV, first.astype(F32), second.astype(F32))


def pack_kernel(ids, z_ref, out):
    bands = []
    for s in range(BANDS):
        n = s * ZBAND + XROWS
        bands.append(
            pick(z_ref[ids[4], n : n + PIECE, :], z_ref[ids[5], n : n + PIECE, :]).astype(BF)
        )
    n = BANDS * ZBAND
    last = pick(z_ref[ids[4], n : n + PIECE, :], z_ref[ids[5], n : n + PIECE, :])
    last = jnp.concatenate([last[:, ROPE:], last[:, ROPE:]], axis=1).astype(BF)
    ropes = [
        jnp.concatenate(
            [z_ref[z, n : n + XROWS, :][:, :ROPE], z_ref[z + NZ // 2, n : n + XROWS, :][:, :ROPE]],
            axis=1,
        )
        for z in range(NZ // 2)
    ]
    for k in range(NX):
        for s in range(BANDS):
            for z in range(NZ):
                first = s * XBAND + z * XROWS
                out[k, first : first + XROWS, :] = z_ref[z, s * ZBAND : s * ZBAND + XROWS, :]
            out[k, s * XBAND + SPAN : (s + 1) * XBAND, :] = bands[s]
        for z in range(NZ // 2):
            out[k, XROPE + z * XROWS : XROPE + (z + 1) * XROWS, :] = ropes[z]
        out[k, XPRE:, :] = last


def column_to_row(col):
    eye = lax.broadcasted_iota(jnp.int32, (128, 128), 0) == lax.broadcasted_iota(
        jnp.int32, (128, 128), 1
    )
    rows = [
        jnp.sum(jnp.where(eye, col[i * 128 : (i + 1) * 128, :], 0.0), axis=0, keepdims=True)
        for i in range(col.shape[0] // 128)
    ]
    return jnp.concatenate(rows, axis=0)


def row_to_column(rows):
    eye = lax.broadcasted_iota(jnp.int32, (128, 128), 0) == lax.broadcasted_iota(
        jnp.int32, (128, 128), 1
    )
    cols = [
        jnp.sum(jnp.where(eye, rows[i : i + 1, :], 0.0), axis=1, keepdims=True)
        for i in range(rows.shape[0])
    ]
    return jnp.concatenate(cols, axis=0)


def three(v):
    high = v.astype(BF).astype(F32)
    mid = (v - high).astype(BF).astype(F32)
    low = v - high - mid
    return [high, mid, low]


def attend_kernel(ids, q0, q1, q2, q3, here, there, wk, wv, out, keys, qfull, att):
    y = ids[0]
    zl = ids[6]
    c = ids[7]
    scale = 1.0 / math.sqrt(QW)
    for i, ref in enumerate((here, there)):
        for j in range(NX):
            n = (i * NX + j) * SPAN
            for s in range(BANDS):
                keys[n : n + SPAN, s * LANES : (s + 1) * LANES] = ref[
                    j, s * XBAND : s * XBAND + SPAN, :
                ]
            ropes = ref[j, XROPE:XPRE, :]
            keys[n : n + SPAN // 2, RANK:] = ropes[:, :ROPE]
            keys[n + SPAN // 2 : n + SPAN, RANK:] = ropes[:, ROPE:]
    for j in range(NX):
        n = NEW + j * PIECE
        for s in range(BANDS + 1):
            first = s * XBAND + SPAN if s < BANDS else XPRE
            mine = here[j, first : first + PIECE, :].astype(F32)
            other = there[j, first : first + PIECE, :].astype(F32)
            band = pick(
                jnp.where(ids[10] == c, mine, other), jnp.where(ids[11] == c, mine, other)
            ).astype(BF)
            if s < BANDS:
                keys[n : n + PIECE, s * LANES : (s + 1) * LANES] = band
            else:
                keys[n : n + PIECE, RANK:] = band[:, :ROPE]
    sources = (q0, q1, q2, q3)
    starts = (0, PAY, PAY, PAY)
    group = NY * TOK
    for h in range(HEADS):
        rows = jnp.concatenate(
            [q[s + h * TOK : s + (h + 1) * TOK, :] for q, s in zip(sources, starts)], axis=0
        )
        k = QROWS + h % (HEADS // 2) * TOK
        ropes = jnp.concatenate([q[s + k : s + k + TOK, :] for q, s in zip(sources, starts)], axis=0)
        ropes = ropes[:, :ROPE] if h < HEADS // 2 else ropes[:, ROPE:]
        absorbed = jnp.dot(rows, wk[h], preferred_element_type=F32).astype(BF)
        full = jnp.concatenate([absorbed, ropes], axis=1)
        qfull[h * group : (h + 1) * group, :] = full

    col = lax.broadcasted_iota(jnp.int32, (1, KEYS), 1)
    zz = lax.rem(lax.div(col, XROWS), NZ)
    xx = lax.rem(lax.div(col, XROWS * NZ), NX)
    cc = lax.div(col, XROWS * NZ * NX)
    cc = jnp.where(cc == 0, c, 1 - c)
    token = zz * (NC * TOK) + cc * TOK + xx * XROWS + lax.rem(col, XROWS) + y * (NZ * NC * TOK)
    token = jnp.where(col < NEW, token, -1)
    row = lax.rem(lax.broadcasted_iota(jnp.int32, (ROWS, 1), 0), group)
    mine = lax.rem(y + lax.div(row, TOK), NY) * (NZ * NC * TOK) + (zl * NC + c) * TOK
    visible = token <= mine + lax.rem(row, TOK)

    def score(i):
        return lax.dot_general(
            qfull[i * ROWS : (i + 1) * ROWS, :],
            keys[...],
            (((1,), (1,)), ((), ())),
            preferred_element_type=F32,
        )

    blocks = NY * QROWS // ROWS
    peaks, totals = [], []
    scores = score(0)
    for i in range(blocks):
        later = score(i + 1) if i + 1 < blocks else None
        scores = jnp.where(visible, scores, NEG)
        peak = jnp.max(scores, axis=1, keepdims=True)
        weights = jnp.exp2((scores - peak) * (scale * math.log2(math.e)))
        total = jnp.sum(weights, axis=1, keepdims=True)
        accum = jnp.dot(weights.astype(BF), keys[:, :RANK], preferred_element_type=F32)
        att[i * ROWS : (i + 1) * ROWS, :] = (accum / total).astype(BF)
        peaks.append(peak * scale)
        totals.append(total)
        scores = later
    stats = three(jnp.concatenate(peaks, axis=0)) + three(jnp.concatenate(totals, axis=0))
    for g in range(NY):
        yq = lax.rem(y + g, NY)
        parts = []
        for v in stats:
            first = [v[h * group + g * TOK : h * group + (g + 1) * TOK] for h in range(HEADS)]
            parts.append(column_to_row(jnp.concatenate(first, axis=0)))
        parts.append(jnp.zeros((STAT - 4 * len(stats), 128), F32))
        out[yq, QROWS:, :] = jnp.concatenate(parts, axis=0).astype(BF)
    for h in range(HEADS):
        mixed = jnp.dot(
            att[h * group : (h + 1) * group, :], wv[h], preferred_element_type=F32
        ).astype(BF)
        for g in range(NY):
            yq = lax.rem(y + g, NY)
            out[yq, h * TOK : (h + 1) * TOK, :] = mixed[g * TOK : (g + 1) * TOK, :]


def merge_kernel(p_ref, out, flat):
    stats = [p_ref[s, QROWS:, :].astype(F32) for s in range(NY)]
    peaks = [v[0:4] + v[4:8] + v[8:12] for v in stats]
    totals = [v[12:16] + v[16:20] + v[20:24] for v in stats]
    peak = functools.reduce(jnp.maximum, peaks)
    weights = [t * jnp.exp(p - peak) for t, p in zip(totals, peaks)]
    total = functools.reduce(jnp.add, weights)
    mixed = sum(
        p_ref[s, 0:QROWS, :].astype(F32) * row_to_column(weights[s] / total) for s in range(NY)
    )
    for h in range(HEADS):
        flat[pl.ds(h, TOK, stride=HEADS), :] = mixed[h * TOK : (h + 1) * TOK, :]
    out[...] = flat[...].reshape(TOK, HEADS, 128).astype(BF)


def on_device(
    hidden, latent_proj, norm_gain, queries, key_absorb, value_absorb, pool_blocks, hit_block
):
    y, zl, c, x = (lax.axis_index(a) for a in ("y", "zl", "c", "x"))
    owner = hit_block // POOL_HERE
    ids = jnp.concatenate(
        [
            jnp.stack([y, x]),
            owner // (NZ * NC),
            (owner // NC) % NZ,
            jnp.stack([zl, c]),
            hit_block % POOL_HERE,
            owner % NC,
        ]
    ).astype(jnp.int32)
    first = HITS * BLOCK + ((y * NZ + zl) * NC + c) * TOK
    positions = (first + jnp.arange(TOK)).astype(F32)
    half = ROPE // 2
    inverse = 10000.0 ** (-jnp.arange(half, dtype=F32) / half)
    angle = positions[:, None] * inverse[None, :]
    cosine, sine = jnp.cos(angle), jnp.sin(angle)
    cosine = jnp.concatenate([cosine, cosine], axis=1)
    sine = jnp.concatenate([-sine, sine], axis=1)

    pay = jax.ShapeDtypeStruct((PAYR, LANES), BF)
    own_q, own_p, p1, p2, p3 = pl.pallas_call(
        prepare_kernel,
        out_shape=[
            jax.ShapeDtypeStruct((PAYR - PAY, LANES), BF),
            jax.ShapeDtypeStruct((PAY, LANES), BF),
            pay,
            pay,
            pay,
        ],
        in_specs=[SMEM] + [VMEM] * 3 + [pl.BlockSpec(memory_space=pltpu.HBM)],
        out_specs=[VMEM] * 5,
        scratch_shapes=[
            pltpu.VMEM((QROWS, 128), F32),
            pltpu.VMEM((QROWS, 128), F32),
            pltpu.VMEM((HITS, WIDTH, BLOCK), BF),
            pltpu.VMEM((HITS * BLOCK, WIDTH), F32),
            pltpu.SemaphoreType.DMA((HITS,)),
        ],
        compiler_params=params(),
        name="prepare",
    )(hit_block, queries, cosine, sine, jnp.swapaxes(pool_blocks, 1, 2))
    received = [
        lax.ppermute(p, "y", [(i, (i - k) % NY) for i in range(NY)])
        for k, p in zip((1, 2, 3), (p1, p2, p3))
    ]

    hidden, own_p = lax.optimization_barrier((hidden, own_p))
    partial = pl.pallas_call(
        project_kernel,
        out_shape=jax.ShapeDtypeStruct((NX, RAWR, LANES), F32),
        in_specs=[VMEM] * 2,
        out_specs=VMEM,
        compiler_params=params(),
        name="project",
    )(hidden, latent_proj.T)
    mine = jnp.sum(lax.all_to_all(partial, "x", 0, 0), axis=0)
    other = lax.ppermute(mine, "zh", [(0, 1), (1, 0)])
    head = pl.BlockSpec((PAY, LANES), lambda i: (0, 0))

    def whole(shape):
        return pl.BlockSpec(shape, lambda i: (0,) * len(shape))

    packed = pl.pallas_call(
        norm_kernel,
        grid=(1,),
        out_shape=jax.ShapeDtypeStruct((NZ, ZROWS, LANES), BF),
        in_specs=[
            SMEM,
            whole((RAWR, LANES)),
            whole((RAWR, LANES)),
            whole((1, RANK)),
            whole((TOK, ROPE)),
            whole((TOK, ROPE)),
            head,
            head,
            head,
            head,
        ],
        out_specs=whole((NZ, ZROWS, LANES)),
        compiler_params=params(),
        name="norm",
    )(ids, mine, other, norm_gain[None, :], cosine, sine, own_p, *received)
    along_z = lax.all_to_all(packed, "zl", 0, 0)
    packed = pl.pallas_call(
        pack_kernel,
        out_shape=jax.ShapeDtypeStruct((NX, CHUNK, LANES), BF),
        in_specs=[SMEM, VMEM],
        out_specs=VMEM,
        compiler_params=params(),
        name="pack",
    )(ids, along_z)
    along_x = lax.all_to_all(packed, "x", 0, 0)
    from_core = lax.ppermute(along_x, "c", [(0, 1), (1, 0)])
    out = pl.pallas_call(
        attend_kernel,
        out_shape=jax.ShapeDtypeStruct((NY, OUTR, 128), BF),
        in_specs=[SMEM] + [VMEM] * 8,
        out_specs=VMEM,
        scratch_shapes=[
            pltpu.VMEM((KEYS, WIDTH), BF),
            pltpu.VMEM((NY * QROWS, WIDTH), BF),
            pltpu.VMEM((NY * QROWS, RANK), BF),
        ],
        compiler_params=params(48),
        name="attend",
    )(ids, own_q, *received, along_x, from_core, key_absorb, value_absorb)
    back = lax.all_to_all(out, "y", 0, 0)
    return pl.pallas_call(
        merge_kernel,
        out_shape=jax.ShapeDtypeStruct((TOK, HEADS, 128), BF),
        in_specs=[VMEM],
        out_specs=VMEM,
        scratch_shapes=[pltpu.VMEM((QROWS, 128), F32)],
        compiler_params=params(),
        name="merge",
    )(back)


def solution(mesh):
    fine = Mesh(mesh.devices.reshape(NY, NZ, NC, NH, NX), CTX + HEAD)
    placed = (
        P(CTX, HEAD),
        P(HEAD, None),
        P(),
        P(CTX, HEAD, None),
        P(HEAD, None, None),
        P(HEAD, None, None),
        P(CTX, None, None),
        P(),
    )
    return jax.shard_map(
        on_device, mesh=fine, in_specs=placed, out_specs=P(CTX, HEAD, None), check_vma=False
    )
```

time: 113 us -> 108 us (0.956)
  blocking collectives: 54.4 us -> 49.1 us
    all_to_all x1 -> x0, blocking collectives: 9.11 us -> none  [on_device(): parts = lax.all_to_all(partial_raw.reshape(NX, XROWS, WIDTH), 'x', 0, 0)]
    all_to_all x0 -> x1, starting transfers between devices: none -> 4.84 us  [on_device(): mine = jnp.sum(lax.all_to_all(partial, 'x', 0, 0), axis=0)]
    ppermute x1, starting transfers between devices: 10.9 us -> 6.96 us  [on_device(): from_core = lax.ppermute(along_x, 'c', [(0, 1), (1, 0)])]
    all_to_all x1, blocking collectives: 22.4 us -> 25 us  [on_device(): along_z = lax.all_to_all(packed, 'zl', 0, 0)]
    pallas_call x2 -> x3, Pallas kernels: 1.41 us -> 3.5 us  [the longest x1 1.68 us: on_device(): pl.pallas_call(prepare_kernel, out_shape=[jax.ShapeDtypeStruct((PAYR - PA...]
    all_to_all x1, blocking collectives: 10.6 us -> 11.8 us  [on_device(): along_x = lax.all_to_all(packed, 'x', 0, 0)]
    unnamed x15 -> x18, local copies, waits for them, and re-layouts: 2.67 us -> 2.69 us
  transfers between devices with their start and end apart: 5 -> 6, of which waited for: 2 -> 2; matrix products, arithmetic and copies ran while one was open for 0% -> 0% of each run, Pallas kernels for 0% -> 0%
where the time goes in v2:
time: 108 us; the launch traced here: 107 us
  blocking collectives  49.1 us (45%)
  starting transfers between devices  36.7 us (34%)
  Pallas kernels  15.3 us (14%)
  waiting for transfers between devices  2.95 us (3%)
  local copies, waits for them, and re-layouts  2.77 us (3%)
    all_to_all x1, blocking collectives, on_device(): along_z = lax.all_to_all(packed, 'zl', 0, 0)  25 us
    ppermute x1, starting transfers between devices, on_device(): other = lax.ppermute(mine, 'zh', [(0, 1), (1, 0)])  15.4 us
    all_to_all x1, blocking collectives, on_device(): back = lax.all_to_all(out, 'y', 0, 0)  12.3 us
    all_to_all x1, blocking collectives, on_device(): along_x = lax.all_to_all(packed, 'x', 0, 0)  11.8 us
    pallas_call x1, Pallas kernels, on_device(): pl.pallas_call(attend_kernel, out_shape=jax.ShapeDtypeStruct((NY, OUTR, 1...  9.73 us
    ppermute x3, starting transfers between devices, on_device(): lax.ppermute(p, 'y', [(i, (i - k) % NY) for i in range(NY)])  9.49 us
    ppermute x1, starting transfers between devices, on_device(): from_core = lax.ppermute(along_x, 'c', [(0, 1), (1, 0)])  6.96 us
    all_to_all x1, starting transfers between devices, on_device(): mine = jnp.sum(lax.all_to_all(partial, 'x', 0, 0), axis=0)  4.84 us
  transfers between devices with their start and end apart: 6, of which 2 were waited for; matrix products, arithmetic and copies ran while one was open for 0% of the time, Pallas kernels for 0%

profile of v2, /device:TPU:1, one launch (start us, length us, event | category | flops | bytes accessed | tf_op | source)
XLA Modules:
  0.0 107.4 jit_solution(6406358954359814870)
XLA Ops:
  0.0 0.0 copy-start.2
  0.0 0.2 fusion
  0.2 0.1 pad_maximum_fusion
  0.3 0.0 copy-start.3
  0.3 1.1 copy-done.3
  1.4 0.0 copy-start.4
  1.4 0.9 copy-done.4
  2.3 0.0 copy-start.7
  2.4 0.7 copy-done.7
  3.0 0.0 copy-start.5
  3.0 1.7 %prepare.1 = (bf16[768,128]{1,0:T(8,128)(2,1)S(1)}, bf16[80,128]{1,0:T(8,128)(2,1)S(1)}, bf16[848,128]{1,0:T(8,128)(2,1)S(1)}, bf16[848,128]{1,0:T(8,128)(2,1)S(1)}, bf16[848,128]{1,0:T(8,128)(2,1)S(1)}) custom-call(s32[2]{0:T(128)S(1)} %copy-done.7, bf16[64,8,192]{2,1,0:T(8,128)(2,1)S(1)} %copy-done.4, f32[64,64]{1,0:T(8,128)S(1)} %get-tuple-element.27.cos_ref, ...), custom_call_target="tpu_custom_call" | custom-call | tf_op jit(solution)/shard_map/prepare/pallas_call | solution.py:353
  4.7 0.0 copy-done.2
  4.7 0.0 copy-done.5
  4.7 1.2 %project.1 = f32[4,72,128]{2,1,0:T(8,128)} custom-call(bf16[64,896]{1,0:T(8,128)(2,1)S(1)} %copy-done.5, bf16[576,896]{1,0:T(8,128)(2,1)S(1)} %bitcast.7), custom_call_target="tpu_custom_call" | custom-call | tf_op jit(solution)/shard_map/project/pallas_call | solution.py:380
  5.9 4.8 %all-to-all-start = ((f32[4,72,128]{2,1,0:T(8,128)}), f32[4,72,128]{2,1,0:T(8,128)S(1)}, u32[]{:S(2)}, u32[]{:S(2)}) async-start(f32[4,72,128]{2,1,0:T(8,128)} %project.1), calls=%async_computation | async-start | bytes 294912 | tf_op jit(solution)/shard_map/all_to_all | solution.py:388
  10.7 4.6 %collective-permute-start = (bf16[848,128]{1,0:T(8,128)(2,1)S(1)}, bf16[848,128]{1,0:T(8,128)(2,1)S(1)}, u32[]{:S(2)}, u32[]{:S(2)}) collective-permute-start(bf16[848,128]{1,0:T(8,128)(2,1)S(1)} %get-tuple-element.13), channel_id=1, source_target_pairs={{0,384},{128,0},{256,128},{384,256},{1,385},{129,1},{257,129},{385... | collective-permute-start | bytes 651272 | tf_op jit(solution)/shard_map/ppermute | solution.py:375
  15.4 0.0 copy-start.8
  15.4 2.3 %collective-permute-start.1 = (bf16[848,128]{1,0:T(8,128)(2,1)S(1)}, bf16[848,128]{1,0:T(8,128)(2,1)S(1)}, u32[]{:S(2)}, u32[]{:S(2)}) collective-permute-start(bf16[848,128]{1,0:T(8,128)(2,1)S(1)} %get-tuple-element.14), channel_id=1, source_target_pairs={{0,256},{128,384},{256,0},{384,128},{1,257},{129,385},{257,1},{385... | collective-permute-start | bytes 651272 | tf_op jit(solution)/shard_map/ppermute | solution.py:375
  17.7 2.6 %collective-permute-start.2 = (bf16[848,128]{1,0:T(8,128)(2,1)S(1)}, bf16[848,128]{1,0:T(8,128)(2,1)S(1)}, u32[]{:S(2)}, u32[]{:S(2)}) collective-permute-start(bf16[848,128]{1,0:T(8,128)(2,1)S(1)} %get-tuple-element.15), channel_id=1, source_target_pairs={{0,128},{128,256},{256,384},{384,0},{1,129},{129,257},{257,385},{3... | collective-permute-start | bytes 651272 | tf_op jit(solution)/shard_map/ppermute | solution.py:375
  20.3 0.0 copy-done.8
  20.3 0.0 all-to-all-done
  20.3 15.4 %collective-permute-start.3 = (f32[72,128]{1,0:T(8,128)S(1)}, f32[72,128]{1,0:T(8,128)S(1)}, u32[]{:S(2)}, u32[]{:S(2)}) collective-permute-start(f32[72,128]{1,0:T(8,128)S(1)} %reduce_sum.9.s_ref), channel_id=1, source_target_pairs={{0,4},{4,0},{1,5},{5,1},{2,6},{6,2},{3,7},{7,3},{8,12},{12,8},{9,1... | collective-permute-start | bytes 110600 | tf_op jit(solution)/shard_map/ppermute | solution.py:389
  35.8 0.0 copy-start.6
  35.8 0.1 concatenate.9.ids
  35.9 1.2 %collective-permute-done.3.r_ref = f32[72,128]{1,0:T(8,128)S(1)} collective-permute-done((f32[72,128]{1,0:T(8,128)S(1)}, f32[72,128]{1,0:T(8,128)S(1)}, u32[]{:S(2)}, u32[]{:S(2)}) %collective-permute-start.3) | collective-permute-done | bytes 36896 | tf_op jit(solution)/shard_map/ppermute | solution.py:389
  37.1 0.0 collective-permute-done.p1.q1
  37.1 0.0 collective-permute-done.1.p2.q2
  37.1 0.0 collective-permute-done.2.p3.q3
  37.1 0.0 copy-done.6
  37.1 0.7 norm.1
  37.8 25.0 %all_to_all.20.z_ref = bf16[8,144,128]{2,1,0:T(8,128)(2,1)S(1)} all-to-all(bf16[8,144,128]{2,1,0:T(8,128)(2,1)S(1)} %norm.1), channel_id=1, replica_groups=mesh['y'=4,'zl'=8,'c'=2,'zh'=2,'x'=4] {'zl'}, dimensions={0} | all-to-all | bytes 589824 | tf_op jit(solution)/shard_map/all_to_all | solution.py:415
  62.8 0.0 copy-start
  62.8 0.0 copy-start.1
  62.8 0.6 pack.1
  63.4 11.8 %all_to_all.21.here = bf16[4,656,128]{2,1,0:T(8,128)(2,1)S(1)} all-to-all(bf16[4,656,128]{2,1,0:T(8,128)(2,1)S(1)} %pack.1), channel_id=1, replica_groups=mesh['y'=4,'zl'=8,'c'=2,'zh'=2,'x'=4] {'x'}, dimensions={0} | all-to-all | bytes 1343488 | tf_op jit(solution)/shard_map/all_to_all | solution.py:424
  75.2 7.0 %collective-permute-start.4 = (bf16[4,656,128]{2,1,0:T(8,128)(2,1)S(1)}, bf16[4,656,128]{2,1,0:T(8,128)(2,1)S(1)}, u32[]{:S(2)}, u32[]{:S(2)}) collective-permute-start(bf16[4,656,128]{2,1,0:T(8,128)(2,1)S(1)} %all_to_all.21.here), channel_id=1, source_target_pairs={{0,8},{8,0},{1,9},{9,1},{2,10},{10,2},{3,11},{11,3},{4,12},{12,4},... | collective-permute-start | bytes 2015240 | tf_op jit(solution)/shard_map/ppermute | solution.py:425
  82.2 1.7 %collective-permute-done.4.there = bf16[4,656,128]{2,1,0:T(8,128)(2,1)S(1)} collective-permute-done((bf16[4,656,128]{2,1,0:T(8,128)(2,1)S(1)}, bf16[4,656,128]{2,1,0:T(8,128)(2,1)S(1)}, u32[]{:S(2)}, u32[]{:S(2)}) %collective-permute-start.4) | collective-permute-done | bytes 671776 | tf_op jit(solution)/shard_map/ppermute | solution.py:425
  83.9 0.0 copy-done
  83.9 0.0 copy-done.1
  83.9 9.7 %attend.1 = bf16[4,544,128]{2,1,0:T(8,128)(2,1)S(1)} custom-call(s32[12]{0:T(128)S(1)} %concatenate.9.ids, bf16[768,128]{1,0:T(8,128)(2,1)S(1)} %get-tuple-element.12.q0, bf16[848,128]{1,0:T(8,128)(2,1)S(1)} %collective-permute-done.p1.q1, bf16[848,128]{1,0:T(8,128)(2,1)S(1)} %collective-permute-done.1.p2.q2, ...), custom_call_target="tpu_custom_call" | custom-call | tf_op jit(solution)/shard_map/attend/pallas_call | solution.py:426
  93.7 12.3 %all_to_all.22.p_ref = bf16[4,544,128]{2,1,0:T(8,128)(2,1)S(1)} all-to-all(bf16[4,544,128]{2,1,0:T(8,128)(2,1)S(1)} %attend.1), channel_id=1, replica_groups=mesh['y'=4,'zl'=8,'c'=2,'zh'=2,'x'=4] {'y'}, dimensions={0} | all-to-all | bytes 1114112 | tf_op jit(solution)/shard_map/all_to_all | solution.py:439
  106.0 1.4 %merge.1 = bf16[64,8,128]{2,1,0:T(8,128)(2,1)} custom-call(bf16[4,544,128]{2,1,0:T(8,128)(2,1)S(1)} %all_to_all.22.p_ref), custom_call_target="tpu_custom_call" | custom-call | tf_op jit(solution)/shard_map/merge/pallas_call | solution.py:440
  (5 shorter events, 0.1 us)
Async XLA Ops:
  0.0 4.7 %copy-start.2 = (bf16[896,576]{0,1:T(8,128)(2,1)S(1)}, bf16[896,576]{0,1:T(8,128)(2,1)}, u32[]{:S(2)}) copy-start(bf16[896,576]{0,1:T(8,128)(2,1)} %param.9) | copy-start | bytes 3096580
  0.3 1.1 copy-start.3
  1.4 0.9 copy-start.4
  2.3 0.7 copy-start.7
  3.0 1.7 %copy-start.5 = (bf16[64,896]{1,0:T(8,128)(2,1)S(1)}, bf16[64,896]{1,0:T(8,128)(2,1)}, u32[]{:S(2)}) copy-start(bf16[64,896]{1,0:T(8,128)(2,1)} %hidden) | copy-start | bytes 344068
  5.9 14.4 %all-to-all-start = ((f32[4,72,128]{2,1,0:T(8,128)}), f32[4,72,128]{2,1,0:T(8,128)S(1)}, u32[]{:S(2)}, u32[]{:S(2)}) async-start(f32[4,72,128]{2,1,0:T(8,128)} %project.1), calls=%async_computation | async-start | bytes 294912 | tf_op jit(solution)/shard_map/all_to_all | solution.py:388
  10.7 26.4 %collective-permute-start = (bf16[848,128]{1,0:T(8,128)(2,1)S(1)}, bf16[848,128]{1,0:T(8,128)(2,1)S(1)}, u32[]{:S(2)}, u32[]{:S(2)}) collective-permute-start(bf16[848,128]{1,0:T(8,128)(2,1)S(1)} %get-tuple-element.13), channel_id=1, source_target_pairs={{0,384},{128,0},{256,128},{384,256},{1,385},{129,1},{257,129},{385... | collective-permute-start | bytes 651272 | tf_op jit(solution)/shard_map/ppermute | solution.py:375
  15.4 4.9 %copy-start.8 = (s32[2]{0:T(128)S(1)}, s32[2]{0:T(128)}, u32[]{:S(2)}) copy-start(s32[2]{0:T(128)} %hit.1) | copy-start | bytes 28
  15.4 21.7 %collective-permute-start.1 = (bf16[848,128]{1,0:T(8,128)(2,1)S(1)}, bf16[848,128]{1,0:T(8,128)(2,1)S(1)}, u32[]{:S(2)}, u32[]{:S(2)}) collective-permute-start(bf16[848,128]{1,0:T(8,128)(2,1)S(1)} %get-tuple-element.14), channel_id=1, source_target_pairs={{0,256},{128,384},{256,0},{384,128},{1,257},{129,385},{257,1},{385... | collective-permute-start | bytes 651272 | tf_op jit(solution)/shard_map/ppermute | solution.py:375
  17.7 19.5 %collective-permute-start.2 = (bf16[848,128]{1,0:T(8,128)(2,1)S(1)}, bf16[848,128]{1,0:T(8,128)(2,1)S(1)}, u32[]{:S(2)}, u32[]{:S(2)}) collective-permute-start(bf16[848,128]{1,0:T(8,128)(2,1)S(1)} %get-tuple-element.15), channel_id=1, source_target_pairs={{0,128},{128,256},{256,384},{384,0},{1,129},{129,257},{257,385},{3... | collective-permute-start | bytes 651272 | tf_op jit(solution)/shard_map/ppermute | solution.py:375
  20.3 16.8 %collective-permute-start.3 = (f32[72,128]{1,0:T(8,128)S(1)}, f32[72,128]{1,0:T(8,128)S(1)}, u32[]{:S(2)}, u32[]{:S(2)}) collective-permute-start(f32[72,128]{1,0:T(8,128)S(1)} %reduce_sum.9.s_ref), channel_id=1, source_target_pairs={{0,4},{4,0},{1,5},{5,1},{2,6},{6,2},{3,7},{7,3},{8,12},{12,8},{9,1... | collective-permute-start | bytes 110600 | tf_op jit(solution)/shard_map/ppermute | solution.py:389
  35.8 1.3 %copy-start.6 = (f32[512]{0:T(512)S(1)}, f32[512]{0:T(512)}, u32[]{:S(2)}) copy-start(f32[512]{0:T(512)} %param.10) | copy-start | bytes 6148
  62.8 21.1 %copy-start = (bf16[8,128,512]{2,1,0:T(8,128)(2,1)S(1)}, bf16[8,128,512]{2,1,0:T(8,128)(2,1)}, u32[]{:S(2)}) copy-start(bf16[8,128,512]{2,1,0:T(8,128)(2,1)} %wk.1) | copy-start | bytes 3145732
  62.8 21.1 %copy-start.1 = (bf16[8,512,128]{2,1,0:T(8,128)(2,1)S(1)}, bf16[8,512,128]{2,1,0:T(8,128)(2,1)}, u32[]{:S(2)}) copy-start(bf16[8,512,128]{2,1,0:T(8,128)(2,1)} %wv.1) | copy-start | bytes 3145732
  75.2 8.7 %collective-permute-start.4 = (bf16[4,656,128]{2,1,0:T(8,128)(2,1)S(1)}, bf16[4,656,128]{2,1,0:T(8,128)(2,1)S(1)}, u32[]{:S(2)}, u32[]{:S(2)}) collective-permute-start(bf16[4,656,128]{2,1,0:T(8,128)(2,1)S(1)} %all_to_all.21.here), channel_id=1, source_target_pairs={{0,8},{8,0},{1,9},{9,1},{2,10},{10,2},{3,11},{11,3},{4,12},{12,4},... | collective-permute-start | bytes 2015240 | tf_op jit(solution)/shard_map/ppermute | solution.py:425

commit v3 on v2

--- a/solution.py
+++ b/solution.py
@@ -32,6 +32,8 @@
 PIECE = HITS * PREV
 QROWS = TOK * HEADS
 LANES = 128
+ATT_MIB = 28
+PROJ_MIB = 62
 BANDS = RANK // LANES
 PAY = (BANDS + 1) * PIECE
 PAYQ = PAY + QROWS
@@ -64,10 +66,8 @@
     return jnp.concatenate([v[:, half:], v[:, :half]], axis=1)
 
 
-def prepare_kernel(
-    hit, q_ref, cos_ref, sin_ref, pool_ref, own_q, own_p, p1, p2, p3, qn, qr, found, pre, sem
-):
-    y, x = lax.axis_index("y"), lax.axis_index("x")
+def prepare_kernel(hit, q_ref, cos_ref, sin_ref, pool_ref, out, qn, qr, found, pre, sem):
+    x = lax.axis_index("x")
     copies = [
         pltpu.make_async_copy(pool_ref.at[lax.rem(hit[b], POOL_HERE)], found.at[b], sem.at[b])
         for b in range(HITS)
@@ -83,28 +83,26 @@
     for h in range(HEADS):
         rope = qr[pl.ds(h, TOK, stride=HEADS), :][:, :ROPE]
         ropes.append(rope * cosine + swap_halves(rope) * sine)
-        out = qn[pl.ds(h, TOK, stride=HEADS), :].astype(BF)
-        own_q[h * TOK : (h + 1) * TOK, :] = out
-        for p in (p1, p2, p3):
-            p[PAY + h * TOK : PAY + (h + 1) * TOK, :] = out
+        rows = qn[pl.ds(h, TOK, stride=HEADS), :].astype(BF)
+        for g in range(NY):
+            out[g, PAY + h * TOK : PAY + (h + 1) * TOK, :] = rows
     for h in range(HEADS // 2):
-        out = jnp.concatenate([ropes[h], ropes[h + HEADS // 2]], axis=1).astype(BF)
-        own_q[QROWS + h * TOK : QROWS + (h + 1) * TOK, :] = out
-        for p in (p1, p2, p3):
-            p[PAYQ + h * TOK : PAYQ + (h + 1) * TOK, :] = out
+        rows = jnp.concatenate([ropes[h], ropes[h + HEADS // 2]], axis=1).astype(BF)
+        for g in range(NY):
+            out[g, PAYQ + h * TOK : PAYQ + (h + 1) * TOK, :] = rows
     for b in range(HITS):
         copies[b].wait()
         pre[b * BLOCK : (b + 1) * BLOCK, :] = found[b].astype(F32).T
-    for shift, p in enumerate((own_p, p1, p2, p3)):
-        target = lax.rem(y - shift + NY, NY)
-        first = x * (BLOCK // NX) + target * PREV
-        piece = jnp.concatenate(
-            [pre[pl.ds(pl.multiple_of(b * BLOCK + first, PREV), PREV), :] for b in range(HITS)],
-            axis=0,
-        )
+    quarter = BLOCK // NX
+    blocks = [
+        pre[pl.ds(pl.multiple_of(b * BLOCK + x * quarter, quarter), quarter), :]
+        for b in range(HITS)
+    ]
+    for g in range(NY):
+        piece = jnp.concatenate([v[g * PREV : (g + 1) * PREV] for v in blocks], axis=0)
         piece = jnp.concatenate([piece, piece[:, RANK:]], axis=1).astype(BF)
         for s in range(BANDS + 1):
-            p[s * PIECE : (s + 1) * PIECE, :] = piece[:, s * LANES : (s + 1) * LANES]
+            out[g, s * PIECE : (s + 1) * PIECE, :] = piece[:, s * LANES : (s + 1) * LANES]
 
 
 def project_kernel(hidden, proj, out):
@@ -120,8 +118,8 @@
         out[k, BANDS * XROWS :, :] = jnp.concatenate([rope[:half], rope[half:]], axis=1)
 
 
-def norm_kernel(ids, s_ref, r_ref, gain_ref, cos_ref, sin_ref, own_p, p1, p2, p3, out):
-    y, x = ids[0], ids[1]
+def norm_kernel(ids, s_ref, r_ref, gain_ref, cos_ref, sin_ref, p_ref, out):
+    x = ids[1]
     raw = s_ref[...] + r_ref[...]
     latent = jnp.concatenate([raw[s * XROWS : (s + 1) * XROWS] for s in range(BANDS)], axis=1)
     rope = raw[BANDS * XROWS :]
@@ -132,20 +130,12 @@
     cosine = cos_ref[pl.ds(start, XROWS), :]
     sine = sin_ref[pl.ds(start, XROWS), :]
     rope = rope * cosine + swap_halves(rope) * sine
-    shifts = [lax.rem(ids[2 + b] - y + NY, NY) for b in range(HITS)]
     row = lax.broadcasted_iota(jnp.int32, (PIECE, LANES), 0)
     bands = []
     for s in range(BANDS + 1):
-        cand = [p[s * PIECE : (s + 1) * PIECE, :].astype(F32) for p in (own_p, p1, p2, p3)]
-        halves = [
-            jnp.where(
-                shift == 0,
-                cand[0],
-                jnp.where(shift == 1, cand[1], jnp.where(shift == 2, cand[2], cand[3])),
-            )
-            for shift in shifts
-        ]
-        bands.append(jnp.where(row < PREV, halves[0], halves[1]))
+        first = p_ref[ids[2], s * PIECE : (s + 1) * PIECE, :].astype(F32)
+        second = p_ref[ids[3], s * PIECE : (s + 1) * PIECE, :].astype(F32)
+        bands.append(jnp.where(row < PREV, first, second))
     ropes = jnp.concatenate([rope, bands[BANDS][:, :ROPE]], axis=1).astype(BF)
     for k in range(NZ):
         for s in range(BANDS):
@@ -217,7 +207,20 @@
     return [high, mid, low]
 
 
-def attend_kernel(ids, q0, q1, q2, q3, here, there, wk, wv, out, keys, qfull, att):
+def absorb_kernel(q_ref, wk, qfull):
+    group = NY * TOK
+    for h in range(HEADS):
+        k = PAY + h * TOK
+        rows = jnp.concatenate([q_ref[g, k : k + TOK, :] for g in range(NY)], axis=0)
+        k = PAYQ + h % (HEADS // 2) * TOK
+        ropes = jnp.concatenate([q_ref[g, k : k + TOK, :] for g in range(NY)], axis=0)
+        ropes = ropes[:, :ROPE] if h < HEADS // 2 else ropes[:, ROPE:]
+        absorbed = jnp.dot(rows, wk[h], preferred_element_type=F32).astype(BF)
+        full = jnp.concatenate([absorbed, ropes], axis=1)
+        qfull[h * group : (h + 1) * group, :] = full
+
+
+def attend_kernel(ids, qfull, here, there, wv, out, keys, att):
     y = ids[0]
     zl = ids[6]
     c = ids[7]
@@ -245,20 +248,7 @@
                 keys[n : n + PIECE, s * LANES : (s + 1) * LANES] = band
             else:
                 keys[n : n + PIECE, RANK:] = band[:, :ROPE]
-    sources = (q0, q1, q2, q3)
-    starts = (0, PAY, PAY, PAY)
     group = NY * TOK
-    for h in range(HEADS):
-        rows = jnp.concatenate(
-            [q[s + h * TOK : s + (h + 1) * TOK, :] for q, s in zip(sources, starts)], axis=0
-        )
-        k = QROWS + h % (HEADS // 2) * TOK
-        ropes = jnp.concatenate([q[s + k : s + k + TOK, :] for q, s in zip(sources, starts)], axis=0)
-        ropes = ropes[:, :ROPE] if h < HEADS // 2 else ropes[:, ROPE:]
-        absorbed = jnp.dot(rows, wk[h], preferred_element_type=F32).astype(BF)
-        full = jnp.concatenate([absorbed, ropes], axis=1)
-        qfull[h * group : (h + 1) * group, :] = full
-
     col = lax.broadcasted_iota(jnp.int32, (1, KEYS), 1)
     zz = lax.rem(lax.div(col, XROWS), NZ)
     xx = lax.rem(lax.div(col, XROWS * NZ), NX)
@@ -267,7 +257,7 @@
     token = zz * (NC * TOK) + cc * TOK + xx * XROWS + lax.rem(col, XROWS) + y * (NZ * NC * TOK)
     token = jnp.where(col < NEW, token, -1)
     row = lax.rem(lax.broadcasted_iota(jnp.int32, (ROWS, 1), 0), group)
-    mine = lax.rem(y + lax.div(row, TOK), NY) * (NZ * NC * TOK) + (zl * NC + c) * TOK
+    mine = lax.div(row, TOK) * (NZ * NC * TOK) + (zl * NC + c) * TOK
     visible = token <= mine + lax.rem(row, TOK)
 
     def score(i):
@@ -294,20 +284,18 @@
         scores = later
     stats = three(jnp.concatenate(peaks, axis=0)) + three(jnp.concatenate(totals, axis=0))
     for g in range(NY):
-        yq = lax.rem(y + g, NY)
         parts = []
         for v in stats:
             first = [v[h * group + g * TOK : h * group + (g + 1) * TOK] for h in range(HEADS)]
             parts.append(column_to_row(jnp.concatenate(first, axis=0)))
         parts.append(jnp.zeros((STAT - 4 * len(stats), 128), F32))
-        out[yq, QROWS:, :] = jnp.concatenate(parts, axis=0).astype(BF)
+        out[g, QROWS:, :] = jnp.concatenate(parts, axis=0).astype(BF)
     for h in range(HEADS):
         mixed = jnp.dot(
             att[h * group : (h + 1) * group, :], wv[h], preferred_element_type=F32
         ).astype(BF)
         for g in range(NY):
-            yq = lax.rem(y + g, NY)
-            out[yq, h * TOK : (h + 1) * TOK, :] = mixed[g * TOK : (g + 1) * TOK, :]
+            out[g, h * TOK : (h + 1) * TOK, :] = mixed[g * TOK : (g + 1) * TOK, :]
 
 
 def merge_kernel(p_ref, out, flat):
@@ -349,18 +337,11 @@
     cosine = jnp.concatenate([cosine, cosine], axis=1)
     sine = jnp.concatenate([-sine, sine], axis=1)
 
-    pay = jax.ShapeDtypeStruct((PAYR, LANES), BF)
-    own_q, own_p, p1, p2, p3 = pl.pallas_call(
+    sent = pl.pallas_call(
         prepare_kernel,
-        out_shape=[
-            jax.ShapeDtypeStruct((PAYR - PAY, LANES), BF),
-            jax.ShapeDtypeStruct((PAY, LANES), BF),
-            pay,
-            pay,
-            pay,
-        ],
+        out_shape=jax.ShapeDtypeStruct((NY, PAYR, LANES), BF),
         in_specs=[SMEM] + [VMEM] * 3 + [pl.BlockSpec(memory_space=pltpu.HBM)],
-        out_specs=[VMEM] * 5,
+        out_specs=VMEM,
         scratch_shapes=[
             pltpu.VMEM((QROWS, 128), F32),
             pltpu.VMEM((QROWS, 128), F32),
@@ -371,24 +352,18 @@
         compiler_params=params(),
         name="prepare",
     )(hit_block, queries, cosine, sine, jnp.swapaxes(pool_blocks, 1, 2))
-    received = [
-        lax.ppermute(p, "y", [(i, (i - k) % NY) for i in range(NY)])
-        for k, p in zip((1, 2, 3), (p1, p2, p3))
-    ]
-
-    hidden, own_p = lax.optimization_barrier((hidden, own_p))
+    received = lax.all_to_all(sent, "y", 0, 0)
+
     partial = pl.pallas_call(
         project_kernel,
         out_shape=jax.ShapeDtypeStruct((NX, RAWR, LANES), F32),
         in_specs=[VMEM] * 2,
         out_specs=VMEM,
-        compiler_params=params(),
+        compiler_params=params(PROJ_MIB),
         name="project",
     )(hidden, latent_proj.T)
     mine = jnp.sum(lax.all_to_all(partial, "x", 0, 0), axis=0)
     other = lax.ppermute(mine, "zh", [(0, 1), (1, 0)])
-    head = pl.BlockSpec((PAY, LANES), lambda i: (0, 0))
-
     def whole(shape):
         return pl.BlockSpec(shape, lambda i: (0,) * len(shape))
 
@@ -403,15 +378,12 @@
             whole((1, RANK)),
             whole((TOK, ROPE)),
             whole((TOK, ROPE)),
-            head,
-            head,
-            head,
-            head,
+            whole((NY, PAY, LANES)),
         ],
         out_specs=whole((NZ, ZROWS, LANES)),
         compiler_params=params(),
         name="norm",
-    )(ids, mine, other, norm_gain[None, :], cosine, sine, own_p, *received)
+    )(ids, mine, other, norm_gain[None, :], cosine, sine, received)
     along_z = lax.all_to_all(packed, "zl", 0, 0)
     packed = pl.pallas_call(
         pack_kernel,
@@ -423,19 +395,26 @@
     )(ids, along_z)
     along_x = lax.all_to_all(packed, "x", 0, 0)
     from_core = lax.ppermute(along_x, "c", [(0, 1), (1, 0)])
+    qfull = pl.pallas_call(
+        absorb_kernel,
+        out_shape=jax.ShapeDtypeStruct((NY * QROWS, WIDTH), BF),
+        in_specs=[VMEM] * 2,
+        out_specs=VMEM,
+        compiler_params=params(16),
+        name="absorb",
+    )(received, key_absorb)
     out = pl.pallas_call(
         attend_kernel,
         out_shape=jax.ShapeDtypeStruct((NY, OUTR, 128), BF),
-        in_specs=[SMEM] + [VMEM] * 8,
+        in_specs=[SMEM] + [VMEM] * 4,
         out_specs=VMEM,
         scratch_shapes=[
             pltpu.VMEM((KEYS, WIDTH), BF),
-            pltpu.VMEM((NY * QROWS, WIDTH), BF),
             pltpu.VMEM((NY * QROWS, RANK), BF),
         ],
-        compiler_params=params(48),
+        compiler_params=params(ATT_MIB),
         name="attend",
-    )(ids, own_q, *received, along_x, from_core, key_absorb, value_absorb)
+    )(ids, qfull, along_x, from_core, value_absorb)
     back = lax.all_to_all(out, "y", 0, 0)
     return pl.pallas_call(
         merge_kernel,

time: 108 us -> 105 us (0.972)
  starting transfers between devices: 36.7 us -> 31.5 us
  Pallas kernels: 15.3 us -> 17.7 us
  blocking collectives: 49.1 us -> 50.2 us
    ppermute x3 -> x0, starting transfers between devices: 9.49 us -> none  [on_device(): lax.ppermute(p, 'y', [(i, (i - k) % NY) for i in range(NY)])]
    all_to_all x0 -> x1, starting transfers between devices: none -> 4.2 us  [on_device(): received = lax.all_to_all(sent, 'y', 0, 0)]
    pallas_call x1 -> x2, Pallas kernels: 1.68 us -> 3.3 us  [the longest x1 2.57 us: on_device(): pl.pallas_call(prepare_kernel, out_shape=jax.ShapeDtypeStruct((NY, PAYR,...]
    pallas_call x1, Pallas kernels: 1.19 us -> 2.49 us  [on_device(): pl.pallas_call(project_kernel, out_shape=jax.ShapeDtypeStruct((NX, RAWR,...]
    unnamed x18 -> x14, local copies, waits for them, and re-layouts: 2.69 us -> 2.68 us
  transfers between devices with their start and end apart: 6 -> 4, of which waited for: 2 -> 2; matrix products, arithmetic and copies ran while one was open for 0% -> 0% of each run, Pallas kernels for 0% -> 3%
where the time goes in v3:
time: 105 us
  blocking collectives  50.2 us (48%)
  starting transfers between devices  31.5 us (30%)
  Pallas kernels  17.7 us (17%)
  local copies, waits for them, and re-layouts  2.76 us (3%)
  waiting for transfers between devices  2.21 us (2%)
    all_to_all x1, blocking collectives, on_device(): along_z = lax.all_to_all(packed, 'zl', 0, 0)  25 us
    ppermute x1, starting transfers between devices, on_device(): other = lax.ppermute(mine, 'zh', [(0, 1), (1, 0)])  15.6 us
    all_to_all x1, blocking collectives, on_device(): back = lax.all_to_all(out, 'y', 0, 0)  13.3 us
    all_to_all x1, blocking collectives, on_device(): along_x = lax.all_to_all(packed, 'x', 0, 0)  11.9 us
    pallas_call x1, Pallas kernels, on_device(): pl.pallas_call(attend_kernel, out_shape=jax.ShapeDtypeStruct((NY, OUTR, 1...  9.19 us
    ppermute x1, starting transfers between devices, on_device(): from_core = lax.ppermute(along_x, 'c', [(0, 1), (1, 0)])  6.9 us
    all_to_all x1, starting transfers between devices, on_device(): mine = jnp.sum(lax.all_to_all(partial, 'x', 0, 0), axis=0)  4.84 us
    all_to_all x1, starting transfers between devices, on_device(): received = lax.all_to_all(sent, 'y', 0, 0)  4.2 us
  transfers between devices with their start and end apart: 4, of which 2 were waited for; matrix products, arithmetic and copies ran while one was open for 0% of the time, Pallas kernels for 3%

profile of v3, /device:TPU:1, one launch (start us, length us, event | category | flops | bytes accessed | tf_op | source)
XLA Modules:
  0.0 104.8 jit_solution(15191483698321009954)
XLA Ops:
  0.0 0.0 copy-start.6
  0.0 0.0 copy-start.4
  0.0 2.5 %project.1 = f32[4,72,128]{2,1,0:T(8,128)} custom-call(bf16[64,896]{1,0:T(8,128)(2,1)} %hidden.1, bf16[576,896]{1,0:T(8,128)(2,1)} %bitcast.9), custom_call_target="tpu_custom_call" | custom-call | tf_op jit(solution)/shard_map/project/pallas_call | solution.py:357
  2.5 4.8 %all-to-all-start.1 = ((f32[4,72,128]{2,1,0:T(8,128)}), f32[4,72,128]{2,1,0:T(8,128)S(1)}, u32[]{:S(2)}, u32[]{:S(2)}) async-start(f32[4,72,128]{2,1,0:T(8,128)} %project.1), calls=%async_computation.1 | async-start | bytes 294912 | tf_op jit(solution)/shard_map/all_to_all | solution.py:365
  7.4 0.2 fusion
  7.6 0.1 pad_maximum_fusion
  7.7 0.0 copy-start.2
  7.7 1.1 %copy-done.2 = bf16[4,128,576]{1,2,0:T(8,128)(2,1)S(1)} copy-done((bf16[4,128,576]{1,2,0:T(8,128)(2,1)S(1)}, bf16[4,128,576]{1,2,0:T(8,128)(2,1)}, u32[]{:S(2)}) %copy-start.2) | copy-done | bytes 589848
  8.7 0.0 copy-start.3
  8.7 0.9 copy-done.3
  9.7 0.0 copy-start.5
  9.7 0.7 copy-done.5
  10.3 2.6 %prepare.1 = bf16[4,848,128]{2,1,0:T(8,128)(2,1)} custom-call(s32[2]{0:T(128)S(1)} %copy-done.5, bf16[64,8,192]{2,1,0:T(8,128)(2,1)S(1)} %copy-done.3, f32[64,64]{1,0:T(8,128)S(1)} %get-tuple-element.13.cos_ref, f32[64,64]{1,0:T(8,128)S(1)} %get-tuple-element.14.sin_ref, bf16[4,576,128]{2,1,0:T(8,128)(2,1)S(1)} %bitcast.7), custom_call_target="tpu_custom_call" | custom-call | tf_op jit(solution)/shard_map/prepare/pallas_call | solution.py:340
  12.9 0.0 all-to-all-done.1
  12.9 4.2 %all-to-all-start = ((bf16[4,848,128]{2,1,0:T(8,128)(2,1)}), bf16[4,848,128]{2,1,0:T(8,128)(2,1)S(1)}, u32[]{:S(2)}, u32[]{:S(2)}) async-start(bf16[4,848,128]{2,1,0:T(8,128)(2,1)} %prepare.1), calls=%async_computation | async-start | bytes 1736704 | tf_op jit(solution)/shard_map/all_to_all | solution.py:355
  17.1 0.0 copy-done.6
  17.1 0.0 copy-start
  17.2 15.6 %collective-permute-start = (f32[72,128]{1,0:T(8,128)S(1)}, f32[72,128]{1,0:T(8,128)S(1)}, u32[]{:S(2)}, u32[]{:S(2)}) collective-permute-start(f32[72,128]{1,0:T(8,128)S(1)} %reduce_sum.9.s_ref), channel_id=1, source_target_pairs={{0,4},{4,0},{1,5},{5,1},{2,6},{6,2},{3,7},{7,3},{8,12},{12,8},{9,1... | collective-permute-start | bytes 110600 | tf_op jit(solution)/shard_map/ppermute | solution.py:366
  32.8 0.1 concatenate.9.ids
  32.8 1.2 %collective-permute-done.r_ref = f32[72,128]{1,0:T(8,128)S(1)} collective-permute-done((f32[72,128]{1,0:T(8,128)S(1)}, f32[72,128]{1,0:T(8,128)S(1)}, u32[]{:S(2)}, u32[]{:S(2)}) %collective-permute-start) | collective-permute-done | bytes 36896 | tf_op jit(solution)/shard_map/ppermute | solution.py:366
  34.1 0.0 all-to-all-done.q_ref.p_ref
  34.1 0.0 copy-done.4
  34.1 0.7 norm.1
  34.8 25.0 %all_to_all.25.z_ref = bf16[8,144,128]{2,1,0:T(8,128)(2,1)S(1)} all-to-all(bf16[8,144,128]{2,1,0:T(8,128)(2,1)S(1)} %norm.1), channel_id=1, replica_groups=mesh['y'=4,'zl'=8,'c'=2,'zh'=2,'x'=4] {'zl'}, dimensions={0} | all-to-all | bytes 589824 | tf_op jit(solution)/shard_map/all_to_all | solution.py:387
  59.7 0.6 pack.1
  60.4 0.0 copy-start.1
  60.4 11.9 %all_to_all.26.here = bf16[4,656,128]{2,1,0:T(8,128)(2,1)S(1)} all-to-all(bf16[4,656,128]{2,1,0:T(8,128)(2,1)S(1)} %pack.1), channel_id=1, replica_groups=mesh['y'=4,'zl'=8,'c'=2,'zh'=2,'x'=4] {'x'}, dimensions={0} | all-to-all | bytes 1343488 | tf_op jit(solution)/shard_map/all_to_all | solution.py:396
  72.3 6.9 %collective-permute-start.1 = (bf16[4,656,128]{2,1,0:T(8,128)(2,1)S(1)}, bf16[4,656,128]{2,1,0:T(8,128)(2,1)S(1)}, u32[]{:S(2)}, u32[]{:S(2)}) collective-permute-start(bf16[4,656,128]{2,1,0:T(8,128)(2,1)S(1)} %all_to_all.26.here), channel_id=1, source_target_pairs={{0,8},{8,0},{1,9},{9,1},{2,10},{10,2},{3,11},{11,3},{4,12},{12,4},... | collective-permute-start | bytes 2015240 | tf_op jit(solution)/shard_map/ppermute | solution.py:397
  79.2 0.0 copy-done
  79.2 0.7 absorb.1.qfull
  79.9 1.0 collective-permute-done.1.there
  80.9 0.0 copy-done.1
  80.9 9.2 %attend.1 = bf16[4,544,128]{2,1,0:T(8,128)(2,1)S(1)} custom-call(s32[12]{0:T(128)S(1)} %concatenate.9.ids, bf16[2048,576]{1,0:T(8,128)(2,1)S(1)} %absorb.1.qfull, bf16[4,656,128]{2,1,0:T(8,128)(2,1)S(1)} %all_to_all.26.here, bf16[4,656,128]{2,1,0:T(8,128)(2,1)S(1)} %collective-permute-done.1.there, bf16[8,512,128]{2,1,0:T(8,128)(2,1)S(1)} %copy-done.1), custom_call_target="tpu_custom_call" | custom-call | tf_op jit(solution)/shard_map/attend/pallas_call | solution.py:406
  90.1 13.3 %all_to_all.27.p_ref = bf16[4,544,128]{2,1,0:T(8,128)(2,1)S(1)} all-to-all(bf16[4,544,128]{2,1,0:T(8,128)(2,1)S(1)} %attend.1), channel_id=1, replica_groups=mesh['y'=4,'zl'=8,'c'=2,'zh'=2,'x'=4] {'y'}, dimensions={0} | all-to-all | bytes 1114112 | tf_op jit(solution)/shard_map/all_to_all | solution.py:418
  103.4 1.4 %merge.1 = bf16[64,8,128]{2,1,0:T(8,128)(2,1)} custom-call(bf16[4,544,128]{2,1,0:T(8,128)(2,1)S(1)} %all_to_all.27.p_ref), custom_call_target="tpu_custom_call" | custom-call | tf_op jit(solution)/shard_map/merge/pallas_call | solution.py:419
  (5 shorter events, 0.1 us)
Async XLA Ops:
  0.0 17.1 %copy-start.6 = (s32[2]{0:T(128)S(1)}, s32[2]{0:T(128)}, u32[]{:S(2)}) copy-start(s32[2]{0:T(128)} %hit.1) | copy-start | bytes 28
  0.0 34.1 %copy-start.4 = (f32[512]{0:T(512)S(1)}, f32[512]{0:T(512)}, u32[]{:S(2)}) copy-start(f32[512]{0:T(512)} %param.10) | copy-start | bytes 6148
  2.5 10.4 %all-to-all-start.1 = ((f32[4,72,128]{2,1,0:T(8,128)}), f32[4,72,128]{2,1,0:T(8,128)S(1)}, u32[]{:S(2)}, u32[]{:S(2)}) async-start(f32[4,72,128]{2,1,0:T(8,128)} %project.1), calls=%async_computation.1 | async-start | bytes 294912 | tf_op jit(solution)/shard_map/all_to_all | solution.py:365
  7.7 1.1 %copy-start.2 = (bf16[4,128,576]{1,2,0:T(8,128)(2,1)S(1)}, bf16[4,128,576]{1,2,0:T(8,128)(2,1)}, u32[]{:S(2)}) copy-start(bf16[4,128,576]{1,2,0:T(8,128)(2,1)} %param.14) | copy-start | bytes 1769476
  8.7 0.9 copy-start.3
  9.7 0.7 copy-start.5
  12.9 21.2 %all-to-all-start = ((bf16[4,848,128]{2,1,0:T(8,128)(2,1)}), bf16[4,848,128]{2,1,0:T(8,128)(2,1)S(1)}, u32[]{:S(2)}, u32[]{:S(2)}) async-start(bf16[4,848,128]{2,1,0:T(8,128)(2,1)} %prepare.1), calls=%async_computation | async-start | bytes 1736704 | tf_op jit(solution)/shard_map/all_to_all | solution.py:355
  17.1 62.1 %copy-start = (bf16[8,128,512]{2,1,0:T(8,128)(2,1)S(1)}, bf16[8,128,512]{2,1,0:T(8,128)(2,1)}, u32[]{:S(2)}) copy-start(bf16[8,128,512]{2,1,0:T(8,128)(2,1)} %wk.1) | copy-start | bytes 3145732
  17.2 16.9 %collective-permute-start = (f32[72,128]{1,0:T(8,128)S(1)}, f32[72,128]{1,0:T(8,128)S(1)}, u32[]{:S(2)}, u32[]{:S(2)}) collective-permute-start(f32[72,128]{1,0:T(8,128)S(1)} %reduce_sum.9.s_ref), channel_id=1, source_target_pairs={{0,4},{4,0},{1,5},{5,1},{2,6},{6,2},{3,7},{7,3},{8,12},{12,8},{9,1... | collective-permute-start | bytes 110600 | tf_op jit(solution)/shard_map/ppermute | solution.py:366
  60.4 20.5 %copy-start.1 = (bf16[8,512,128]{2,1,0:T(8,128)(2,1)S(1)}, bf16[8,512,128]{2,1,0:T(8,128)(2,1)}, u32[]{:S(2)}) copy-start(bf16[8,512,128]{2,1,0:T(8,128)(2,1)} %wv.1) | copy-start | bytes 3145732
  72.3 8.6 %collective-permute-start.1 = (bf16[4,656,128]{2,1,0:T(8,128)(2,1)S(1)}, bf16[4,656,128]{2,1,0:T(8,128)(2,1)S(1)}, u32[]{:S(2)}, u32[]{:S(2)}) collective-permute-start(bf16[4,656,128]{2,1,0:T(8,128)(2,1)S(1)} %all_to_all.26.here), channel_id=1, source_target_pairs={{0,8},{8,0},{1,9},{9,1},{2,10},{10,2},{3,11},{11,3},{4,12},{12,4},... | collective-permute-start | bytes 2015240 | tf_op jit(solution)/shard_map/ppermute | solution.py:397

commit v4 on v3

--- a/solution.py
+++ b/solution.py
@@ -14,7 +14,8 @@
 F32 = jnp.float32
 
 NY, NZ, NC, NH, NX = 4, 8, 2, 2, 4
-CTX = ("y", "zl", "c")
+NR = NZ // 2
+CTX = ("y", "zq", "zr", "c")
 HEAD = ("zh", "x")
 
 TOK = 64
@@ -41,6 +42,11 @@
 RAWR = BANDS * XROWS + XROWS // 2
 ZBAND = XROWS + PIECE
 ZROWS = BANDS * ZBAND + 16
+HALF = NR * XROWS
+HBAND = HALF + PIECE
+HROPE = BANDS * HBAND
+HPRE = HROPE + HALF // 2
+HROWS = HPRE + PIECE
 SPAN = NZ * XROWS
 XBAND = SPAN + PIECE
 XROPE = BANDS * XBAND
@@ -137,7 +143,7 @@
         second = p_ref[ids[3], s * PIECE : (s + 1) * PIECE, :].astype(F32)
         bands.append(jnp.where(row < PREV, first, second))
     ropes = jnp.concatenate([rope, bands[BANDS][:, :ROPE]], axis=1).astype(BF)
-    for k in range(NZ):
+    for k in range(NR):
         for s in range(BANDS):
             n = s * ZBAND
             out[k, n : n + XROWS, :] = scaled[:, s * LANES : (s + 1) * LANES]
@@ -150,31 +156,45 @@
     return jnp.where(row < PREV, first.astype(F32), second.astype(F32))
 
 
-def pack_kernel(ids, z_ref, out):
-    bands = []
+def half_kernel(ids, z_ref, out):
+    first, second = lax.rem(ids[4], NR), lax.rem(ids[5], NR)
+    n = BANDS * ZBAND
     for s in range(BANDS):
-        n = s * ZBAND + XROWS
-        bands.append(
-            pick(z_ref[ids[4], n : n + PIECE, :], z_ref[ids[5], n : n + PIECE, :]).astype(BF)
+        for k in range(NR):
+            m = s * HBAND + k * XROWS
+            out[m : m + XROWS, :] = z_ref[k, s * ZBAND : s * ZBAND + XROWS, :]
+        m = s * ZBAND + XROWS
+        band = pick(z_ref[first, m : m + PIECE, :], z_ref[second, m : m + PIECE, :])
+        out[s * HBAND + HALF : (s + 1) * HBAND, :] = band.astype(BF)
+    for k in range(NR // 2):
+        m = HROPE + k * XROWS
+        out[m : m + XROWS, :] = jnp.concatenate(
+            [z_ref[i, n : n + XROWS, :][:, :ROPE] for i in (k, k + NR // 2)], axis=1
         )
-    n = BANDS * ZBAND
-    last = pick(z_ref[ids[4], n : n + PIECE, :], z_ref[ids[5], n : n + PIECE, :])
-    last = jnp.concatenate([last[:, ROPE:], last[:, ROPE:]], axis=1).astype(BF)
-    ropes = [
-        jnp.concatenate(
-            [z_ref[z, n : n + XROWS, :][:, :ROPE], z_ref[z + NZ // 2, n : n + XROWS, :][:, :ROPE]],
-            axis=1,
-        )
-        for z in range(NZ // 2)
-    ]
+    band = pick(z_ref[first, n : n + PIECE, :], z_ref[second, n : n + PIECE, :])
+    out[HPRE:, :] = jnp.concatenate([band[:, ROPE:], band[:, ROPE:]], axis=1).astype(BF)
+
+
+def pack_kernel(ids, own, other, out):
+    quad = lax.div(ids[6], NR)
+    mine = [lax.div(ids[4 + b], NR) == quad for b in range(HITS)]
+
+    def piece(m):
+        a = own[m : m + PIECE, :].astype(F32)
+        b = other[m : m + PIECE, :].astype(F32)
+        return pick(*[jnp.where(here, a, b) for here in mine]).astype(BF)
+
+    bands = [piece(s * HBAND + HALF) for s in range(BANDS)]
+    last = piece(HPRE)
     for k in range(NX):
+        for i, ref in enumerate((own, other)):
+            for s in range(BANDS):
+                n = s * XBAND + i * HALF
+                out[k, n : n + HALF, :] = ref[s * HBAND : s * HBAND + HALF, :]
+            n = XROPE + i * (HALF // 2)
+            out[k, n : n + HALF // 2, :] = ref[HROPE:HPRE, :]
         for s in range(BANDS):
-            for z in range(NZ):
-                first = s * XBAND + z * XROWS
-                out[k, first : first + XROWS, :] = z_ref[z, s * ZBAND : s * ZBAND + XROWS, :]
             out[k, s * XBAND + SPAN : (s + 1) * XBAND, :] = bands[s]
-        for z in range(NZ // 2):
-            out[k, XROPE + z * XROWS : XROPE + (z + 1) * XROWS, :] = ropes[z]
         out[k, XPRE:, :] = last
 
 
@@ -233,8 +253,11 @@
                     j, s * XBAND : s * XBAND + SPAN, :
                 ]
             ropes = ref[j, XROPE:XPRE, :]
-            keys[n : n + SPAN // 2, RANK:] = ropes[:, :ROPE]
-            keys[n + SPAN // 2 : n + SPAN, RANK:] = ropes[:, ROPE:]
+            for k in range(4):
+                m = k // 2 * (HALF // 2)
+                part = ropes[m : m + HALF // 2]
+                part = part[:, :ROPE] if k % 2 == 0 else part[:, ROPE:]
+                keys[n + k * (HALF // 2) : n + (k + 1) * (HALF // 2), RANK:] = part
     for j in range(NX):
         n = NEW + j * PIECE
         for s in range(BANDS + 1):
@@ -250,7 +273,9 @@
                 keys[n : n + PIECE, RANK:] = band[:, :ROPE]
     group = NY * TOK
     col = lax.broadcasted_iota(jnp.int32, (1, KEYS), 1)
-    zz = lax.rem(lax.div(col, XROWS), NZ)
+    slot = lax.rem(lax.div(col, XROWS), NZ)
+    quad = lax.div(zl, NR)
+    zz = jnp.where(slot < NR, quad, 1 - quad) * NR + lax.rem(slot, NR)
     xx = lax.rem(lax.div(col, XROWS * NZ), NX)
     cc = lax.div(col, XROWS * NZ * NX)
     cc = jnp.where(cc == 0, c, 1 - c)
@@ -313,10 +338,24 @@
     out[...] = flat[...].reshape(TOK, HEADS, 128).astype(BF)
 
 
+def mirrored():
+    ring = NH * NZ
+
+    def index(r):
+        return r % NZ * NH + r // NZ
+
+    pairs = []
+    for r in range(ring):
+        first, offset = r // NR * NR, r % NR
+        partner = first - 1 - offset if offset < NR // 2 else first + 2 * NR - 1 - offset
+        pairs.append((index(r), index(partner % ring)))
+    return pairs
+
+
 def on_device(
     hidden, latent_proj, norm_gain, queries, key_absorb, value_absorb, pool_blocks, hit_block
 ):
-    y, zl, c, x = (lax.axis_index(a) for a in ("y", "zl", "c", "x"))
+    y, zl, c, x = (lax.axis_index(a) for a in ("y", ("zq", "zr"), "c", "x"))
     owner = hit_block // POOL_HERE
     ids = jnp.concatenate(
         [
@@ -370,7 +409,7 @@
     packed = pl.pallas_call(
         norm_kernel,
         grid=(1,),
-        out_shape=jax.ShapeDtypeStruct((NZ, ZROWS, LANES), BF),
+        out_shape=jax.ShapeDtypeStruct((NR, ZROWS, LANES), BF),
         in_specs=[
             SMEM,
             whole((RAWR, LANES)),
@@ -380,19 +419,28 @@
             whole((TOK, ROPE)),
             whole((NY, PAY, LANES)),
         ],
-        out_specs=whole((NZ, ZROWS, LANES)),
+        out_specs=whole((NR, ZROWS, LANES)),
         compiler_params=params(),
         name="norm",
     )(ids, mine, other, norm_gain[None, :], cosine, sine, received)
-    along_z = lax.all_to_all(packed, "zl", 0, 0)
+    quad = lax.all_to_all(packed, "zr", 0, 0)
+    half = pl.pallas_call(
+        half_kernel,
+        out_shape=jax.ShapeDtypeStruct((HROWS, LANES), BF),
+        in_specs=[SMEM, VMEM],
+        out_specs=VMEM,
+        compiler_params=params(),
+        name="half",
+    )(ids, quad)
+    other_half = lax.ppermute(half, ("zq", "zr", "zh"), mirrored())
     packed = pl.pallas_call(
         pack_kernel,
         out_shape=jax.ShapeDtypeStruct((NX, CHUNK, LANES), BF),
-        in_specs=[SMEM, VMEM],
+        in_specs=[SMEM] + [VMEM] * 2,
         out_specs=VMEM,
         compiler_params=params(),
         name="pack",
-    )(ids, along_z)
+    )(ids, half, other_half)
     along_x = lax.all_to_all(packed, "x", 0, 0)
     from_core = lax.ppermute(along_x, "c", [(0, 1), (1, 0)])
     qfull = pl.pallas_call(
@@ -428,7 +476,7 @@
 
 
 def solution(mesh):
-    fine = Mesh(mesh.devices.reshape(NY, NZ, NC, NH, NX), CTX + HEAD)
+    fine = Mesh(mesh.devices.reshape(NY, NZ // NR, NR, NC, NH, NX), CTX + HEAD)
     placed = (
         P(CTX, HEAD),
         P(HEAD, None),

time: 105 us -> 101 us (0.962)
  blocking collectives: 50.2 us -> 33.6 us
  starting transfers between devices: 31.5 us -> 40 us
  waiting for transfers between devices: 2.21 us -> 5.16 us
    all_to_all x1, blocking collectives: 25 us -> 8.24 us  [on_device(): quad = lax.all_to_all(packed, 'zr', 0, 0)]
    ppermute x0 -> x1, starting transfers between devices: none -> 6.93 us  [on_device(): other_half = lax.ppermute(half, ('zq', 'zr', 'zh'), mirrored())]
    ppermute x0 -> x1, waiting for transfers between devices: none -> 2.96 us  [on_device(): other_half = lax.ppermute(half, ('zq', 'zr', 'zh'), mirrored())]
    ppermute x1, starting transfers between devices: 6.9 us -> 8.48 us  [on_device(): from_core = lax.ppermute(along_x, 'c', [(0, 1), (1, 0)])]
  transfers between devices with their start and end apart: 4 -> 5, of which waited for: 2 -> 3; matrix products, arithmetic and copies ran while one was open for 0% -> 0% of each run, Pallas kernels for 3% -> 3%
where the time goes in v4:
time: 101 us
  starting transfers between devices  40 us (40%)
  blocking collectives  33.6 us (33%)
  Pallas kernels  18.5 us (18%)
  waiting for transfers between devices  5.16 us (5%)
  local copies, waits for them, and re-layouts  2.76 us (3%)
    ppermute x1, starting transfers between devices, on_device(): other = lax.ppermute(mine, 'zh', [(0, 1), (1, 0)])  15.4 us
    all_to_all x1, blocking collectives, on_device(): back = lax.all_to_all(out, 'y', 0, 0)  13.6 us
    all_to_all x1, blocking collectives, on_device(): along_x = lax.all_to_all(packed, 'x', 0, 0)  11.8 us
    pallas_call x1, Pallas kernels, on_device(): pl.pallas_call(attend_kernel, out_shape=jax.ShapeDtypeStruct((NY, OUTR, 1...  9.44 us
    ppermute x1, starting transfers between devices, on_device(): from_core = lax.ppermute(along_x, 'c', [(0, 1), (1, 0)])  8.48 us
    all_to_all x1, blocking collectives, on_device(): quad = lax.all_to_all(packed, 'zr', 0, 0)  8.24 us
    ppermute x1, starting transfers between devices, on_device(): other_half = lax.ppermute(half, ('zq', 'zr', 'zh'), mirrored())  6.93 us
    all_to_all x1, starting transfers between devices, on_device(): mine = jnp.sum(lax.all_to_all(partial, 'x', 0, 0), axis=0)  4.84 us
  transfers between devices with their start and end apart: 5, of which 3 were waited for; matrix products, arithmetic and copies ran while one was open for 0% of the time, Pallas kernels for 3%

profile of v4, /device:TPU:1, one launch (start us, length us, event | category | flops | bytes accessed | tf_op | source)
XLA Modules:
  0.0 100.6 jit_solution(17008757332503927121)
XLA Ops:
  0.0 0.0 copy-start.6
  0.0 0.0 copy-start.4
  0.0 2.5 %project.1 = f32[4,72,128]{2,1,0:T(8,128)} custom-call(bf16[64,896]{1,0:T(8,128)(2,1)} %hidden.1, bf16[576,896]{1,0:T(8,128)(2,1)} %bitcast.9), custom_call_target="tpu_custom_call" | custom-call | tf_op jit(solution)/shard_map/project/pallas_call | solution.py:396
  2.5 4.8 %all-to-all-start.1 = ((f32[4,72,128]{2,1,0:T(8,128)}), f32[4,72,128]{2,1,0:T(8,128)S(1)}, u32[]{:S(2)}, u32[]{:S(2)}) async-start(f32[4,72,128]{2,1,0:T(8,128)} %project.1), calls=%async_computation.1 | async-start | bytes 294912 | tf_op jit(solution)/shard_map/all_to_all | solution.py:404
  7.4 0.2 fusion
  7.6 0.1 pad_maximum_fusion
  7.7 0.0 copy-start.2
  7.7 1.1 %copy-done.2 = bf16[4,128,576]{1,2,0:T(8,128)(2,1)S(1)} copy-done((bf16[4,128,576]{1,2,0:T(8,128)(2,1)S(1)}, bf16[4,128,576]{1,2,0:T(8,128)(2,1)}, u32[]{:S(2)}) %copy-start.2) | copy-done | bytes 589848
  8.7 0.0 copy-start.3
  8.7 0.9 copy-done.3
  9.7 0.0 copy-start.5
  9.7 0.7 copy-done.5
  10.3 2.6 %prepare.1 = bf16[4,848,128]{2,1,0:T(8,128)(2,1)} custom-call(s32[2]{0:T(128)S(1)} %copy-done.5, bf16[64,8,192]{2,1,0:T(8,128)(2,1)S(1)} %copy-done.3, f32[64,64]{1,0:T(8,128)S(1)} %get-tuple-element.13.cos_ref, f32[64,64]{1,0:T(8,128)S(1)} %get-tuple-element.14.sin_ref, bf16[4,576,128]{2,1,0:T(8,128)(2,1)S(1)} %bitcast.7), custom_call_target="tpu_custom_call" | custom-call | tf_op jit(solution)/shard_map/prepare/pallas_call | solution.py:379
  12.9 0.0 copy-start
  12.9 0.0 all-to-all-done.1
  12.9 4.3 %all-to-all-start = ((bf16[4,848,128]{2,1,0:T(8,128)(2,1)}), bf16[4,848,128]{2,1,0:T(8,128)(2,1)S(1)}, u32[]{:S(2)}, u32[]{:S(2)}) async-start(bf16[4,848,128]{2,1,0:T(8,128)(2,1)} %prepare.1), calls=%async_computation | async-start | bytes 1736704 | tf_op jit(solution)/shard_map/all_to_all | solution.py:394
  17.2 0.0 copy-done.6
  17.3 15.4 %collective-permute-start = (f32[72,128]{1,0:T(8,128)S(1)}, f32[72,128]{1,0:T(8,128)S(1)}, u32[]{:S(2)}, u32[]{:S(2)}) collective-permute-start(f32[72,128]{1,0:T(8,128)S(1)} %reduce_sum.9.s_ref), channel_id=1, source_target_pairs={{0,4},{4,0},{1,5},{5,1},{2,6},{6,2},{3,7},{7,3},{8,12},{12,8},{9,1... | collective-permute-start | bytes 110600 | tf_op jit(solution)/shard_map/ppermute | solution.py:405
  32.8 0.1 concatenate.9.ids
  32.8 1.2 %collective-permute-done.r_ref = f32[72,128]{1,0:T(8,128)S(1)} collective-permute-done((f32[72,128]{1,0:T(8,128)S(1)}, f32[72,128]{1,0:T(8,128)S(1)}, u32[]{:S(2)}, u32[]{:S(2)}) %collective-permute-start) | collective-permute-done | bytes 36896 | tf_op jit(solution)/shard_map/ppermute | solution.py:405
  34.1 0.0 all-to-all-done.q_ref.p_ref
  34.1 0.0 copy-done.4
  34.1 0.7 norm.1
  34.7 8.2 %all_to_all.25.z_ref = bf16[4,144,128]{2,1,0:T(8,128)(2,1)S(1)} all-to-all(bf16[4,144,128]{2,1,0:T(8,128)(2,1)S(1)} %norm.1), channel_id=1, replica_groups=mesh['y'=4,'zq'=2,'zr'=4,'c'=2,'zh'=2,'x'=4] {'zr'}, dimensions={0} | all-to-all | bytes 294912 | tf_op jit(solution)/shard_map/all_to_all | solution.py:426
  43.0 0.6 half.1.own
  43.6 6.9 %collective-permute-start.1 = (bf16[368,128]{1,0:T(8,128)(2,1)S(1)}, bf16[368,128]{1,0:T(8,128)(2,1)S(1)}, u32[]{:S(2)}, u32[]{:S(2)}) collective-permute-start(bf16[368,128]{1,0:T(8,128)(2,1)S(1)} %half.1.own), channel_id=1, source_target_pairs={{0,116},{16,100},{32,80},{48,64},{64,48},{80,32},{96,20},{112,4},{... | collective-permute-start | bytes 282632 | tf_op jit(solution)/shard_map/ppermute | solution.py:435
  50.5 3.0 %collective-permute-done.1.other = bf16[368,128]{1,0:T(8,128)(2,1)S(1)} collective-permute-done((bf16[368,128]{1,0:T(8,128)(2,1)S(1)}, bf16[368,128]{1,0:T(8,128)(2,1)S(1)}, u32[]{:S(2)}, u32[]{:S(2)}) %collective-permute-start.1) | collective-permute-done | bytes 94240 | tf_op jit(solution)/shard_map/ppermute | solution.py:435
  53.5 0.6 pack.1
  54.1 0.0 copy-start.1
  54.1 11.8 %all_to_all.26.here = bf16[4,656,128]{2,1,0:T(8,128)(2,1)S(1)} all-to-all(bf16[4,656,128]{2,1,0:T(8,128)(2,1)S(1)} %pack.1), channel_id=1, replica_groups=mesh['y'=4,'zq'=2,'zr'=4,'c'=2,'zh'=2,'x'=4] {'x'}, dimensions={0} | all-to-all | bytes 1343488 | tf_op jit(solution)/shard_map/all_to_all | solution.py:444
  66.0 8.5 %collective-permute-start.2 = (bf16[4,656,128]{2,1,0:T(8,128)(2,1)S(1)}, bf16[4,656,128]{2,1,0:T(8,128)(2,1)S(1)}, u32[]{:S(2)}, u32[]{:S(2)}) collective-permute-start(bf16[4,656,128]{2,1,0:T(8,128)(2,1)S(1)} %all_to_all.26.here), channel_id=1, source_target_pairs={{0,8},{8,0},{1,9},{9,1},{2,10},{10,2},{3,11},{11,3},{4,12},{12,4},... | collective-permute-start | bytes 2015240 | tf_op jit(solution)/shard_map/ppermute | solution.py:445
  74.5 0.0 copy-done
  74.5 0.7 absorb.1.qfull
  75.2 1.0 collective-permute-done.2.there
  76.2 0.0 copy-done.1
  76.2 9.4 %attend.1 = bf16[4,544,128]{2,1,0:T(8,128)(2,1)S(1)} custom-call(s32[12]{0:T(128)S(1)} %concatenate.9.ids, bf16[2048,576]{1,0:T(8,128)(2,1)S(1)} %absorb.1.qfull, bf16[4,656,128]{2,1,0:T(8,128)(2,1)S(1)} %all_to_all.26.here, bf16[4,656,128]{2,1,0:T(8,128)(2,1)S(1)} %collective-permute-done.2.there, bf16[8,512,128]{2,1,0:T(8,128)(2,1)S(1)} %copy-done.1), custom_call_target="tpu_custom_call" | custom-call | tf_op jit(solution)/shard_map/attend/pallas_call | solution.py:454
  85.6 13.6 %all_to_all.27.p_ref = bf16[4,544,128]{2,1,0:T(8,128)(2,1)S(1)} all-to-all(bf16[4,544,128]{2,1,0:T(8,128)(2,1)S(1)} %attend.1), channel_id=1, replica_groups=mesh['y'=4,'zq'=2,'zr'=4,'c'=2,'zh'=2,'x'=4] {'y'}, dimensions={0} | all-to-all | bytes 1114112 | tf_op jit(solution)/shard_map/all_to_all | solution.py:466
  99.2 1.4 %merge.1 = bf16[64,8,128]{2,1,0:T(8,128)(2,1)} custom-call(bf16[4,544,128]{2,1,0:T(8,128)(2,1)S(1)} %all_to_all.27.p_ref), custom_call_target="tpu_custom_call" | custom-call | tf_op jit(solution)/shard_map/merge/pallas_call | solution.py:467
  (5 shorter events, 0.1 us)
Async XLA Ops:
  0.0 17.2 %copy-start.6 = (s32[2]{0:T(128)S(1)}, s32[2]{0:T(128)}, u32[]{:S(2)}) copy-start(s32[2]{0:T(128)} %hit.1) | copy-start | bytes 28
  0.0 34.1 %copy-start.4 = (f32[512]{0:T(512)S(1)}, f32[512]{0:T(512)}, u32[]{:S(2)}) copy-start(f32[512]{0:T(512)} %param.10) | copy-start | bytes 6148
  2.5 10.4 %all-to-all-start.1 = ((f32[4,72,128]{2,1,0:T(8,128)}), f32[4,72,128]{2,1,0:T(8,128)S(1)}, u32[]{:S(2)}, u32[]{:S(2)}) async-start(f32[4,72,128]{2,1,0:T(8,128)} %project.1), calls=%async_computation.1 | async-start | bytes 294912 | tf_op jit(solution)/shard_map/all_to_all | solution.py:404
  7.7 1.1 %copy-start.2 = (bf16[4,128,576]{1,2,0:T(8,128)(2,1)S(1)}, bf16[4,128,576]{1,2,0:T(8,128)(2,1)}, u32[]{:S(2)}) copy-start(bf16[4,128,576]{1,2,0:T(8,128)(2,1)} %param.14) | copy-start | bytes 1769476
  8.7 0.9 copy-start.3
  9.7 0.7 copy-start.5
  12.9 61.6 %copy-start = (bf16[8,128,512]{2,1,0:T(8,128)(2,1)S(1)}, bf16[8,128,512]{2,1,0:T(8,128)(2,1)}, u32[]{:S(2)}) copy-start(bf16[8,128,512]{2,1,0:T(8,128)(2,1)} %wk.1) | copy-start | bytes 3145732
  12.9 21.1 %all-to-all-start = ((bf16[4,848,128]{2,1,0:T(8,128)(2,1)}), bf16[4,848,128]{2,1,0:T(8,128)(2,1)S(1)}, u32[]{:S(2)}, u32[]{:S(2)}) async-start(bf16[4,848,128]{2,1,0:T(8,128)(2,1)} %prepare.1), calls=%async_computation | async-start | bytes 1736704 | tf_op jit(solution)/shard_map/all_to_all | solution.py:394
  17.3 16.8 %collective-permute-start = (f32[72,128]{1,0:T(8,128)S(1)}, f32[72,128]{1,0:T(8,128)S(1)}, u32[]{:S(2)}, u32[]{:S(2)}) collective-permute-start(f32[72,128]{1,0:T(8,128)S(1)} %reduce_sum.9.s_ref), channel_id=1, source_target_pairs={{0,4},{4,0},{1,5},{5,1},{2,6},{6,2},{3,7},{7,3},{8,12},{12,8},{9,1... | collective-permute-start | bytes 110600 | tf_op jit(solution)/shard_map/ppermute | solution.py:405
  43.6 9.9 %collective-permute-start.1 = (bf16[368,128]{1,0:T(8,128)(2,1)S(1)}, bf16[368,128]{1,0:T(8,128)(2,1)S(1)}, u32[]{:S(2)}, u32[]{:S(2)}) collective-permute-start(bf16[368,128]{1,0:T(8,128)(2,1)S(1)} %half.1.own), channel_id=1, source_target_pairs={{0,116},{16,100},{32,80},{48,64},{64,48},{80,32},{96,20},{112,4},{... | collective-permute-start | bytes 282632 | tf_op jit(solution)/shard_map/ppermute | solution.py:435
  54.1 22.1 %copy-start.1 = (bf16[8,512,128]{2,1,0:T(8,128)(2,1)S(1)}, bf16[8,512,128]{2,1,0:T(8,128)(2,1)}, u32[]{:S(2)}) copy-start(bf16[8,512,128]{2,1,0:T(8,128)(2,1)} %wv.1) | copy-start | bytes 3145732
  66.0 10.2 %collective-permute-start.2 = (bf16[4,656,128]{2,1,0:T(8,128)(2,1)S(1)}, bf16[4,656,128]{2,1,0:T(8,128)(2,1)S(1)}, u32[]{:S(2)}, u32[]{:S(2)}) collective-permute-start(bf16[4,656,128]{2,1,0:T(8,128)(2,1)S(1)} %all_to_all.26.here), channel_id=1, source_target_pairs={{0,8},{8,0},{1,9},{9,1},{2,10},{10,2},{3,11},{11,3},{4,12},{12,4},... | collective-permute-start | bytes 2015240 | tf_op jit(solution)/shard_map/ppermute | solution.py:445

commit v5 on v4

--- a/solution.py
+++ b/solution.py
@@ -196,28 +196,6 @@
         for s in range(BANDS):
             out[k, s * XBAND + SPAN : (s + 1) * XBAND, :] = bands[s]
         out[k, XPRE:, :] = last
-
-
-def column_to_row(col):
-    eye = lax.broadcasted_iota(jnp.int32, (128, 128), 0) == lax.broadcasted_iota(
-        jnp.int32, (128, 128), 1
-    )
-    rows = [
-        jnp.sum(jnp.where(eye, col[i * 128 : (i + 1) * 128, :], 0.0), axis=0, keepdims=True)
-        for i in range(col.shape[0] // 128)
-    ]
-    return jnp.concatenate(rows, axis=0)
-
-
-def row_to_column(rows):
-    eye = lax.broadcasted_iota(jnp.int32, (128, 128), 0) == lax.broadcasted_iota(
-        jnp.int32, (128, 128), 1
-    )
-    cols = [
-        jnp.sum(jnp.where(eye, rows[i : i + 1, :], 0.0), axis=1, keepdims=True)
-        for i in range(rows.shape[0])
-    ]
-    return jnp.concatenate(cols, axis=0)
 
 
 def three(v):
@@ -308,11 +286,16 @@
         totals.append(total)
         scores = later
     stats = three(jnp.concatenate(peaks, axis=0)) + three(jnp.concatenate(totals, axis=0))
+    blank = jnp.zeros((NY * QROWS, 8 - len(stats)), F32)
+    table = jnp.concatenate(stats + [blank], axis=1)
     for g in range(NY):
-        parts = []
-        for v in stats:
-            first = [v[h * group + g * TOK : h * group + (g + 1) * TOK] for h in range(HEADS)]
-            parts.append(column_to_row(jnp.concatenate(first, axis=0)))
+        first = [table[h * group + g * TOK : h * group + (g + 1) * TOK] for h in range(HEADS)]
+        turned = jnp.concatenate(first, axis=0).T
+        parts = [
+            turned[k : k + 1, i * LANES : (i + 1) * LANES]
+            for k in range(len(stats))
+            for i in range(QROWS // LANES)
+        ]
         parts.append(jnp.zeros((STAT - 4 * len(stats), 128), F32))
         out[g, QROWS:, :] = jnp.concatenate(parts, axis=0).astype(BF)
     for h in range(HEADS):
@@ -330,9 +313,13 @@
     peak = functools.reduce(jnp.maximum, peaks)
     weights = [t * jnp.exp(p - peak) for t, p in zip(totals, peaks)]
     total = functools.reduce(jnp.add, weights)
-    mixed = sum(
-        p_ref[s, 0:QROWS, :].astype(F32) * row_to_column(weights[s] / total) for s in range(NY)
-    )
+    share = jnp.concatenate([w / total for w in weights], axis=0).T
+    bands = QROWS // LANES
+    columns = [
+        jnp.concatenate([share[:, s * bands + i :][:, :1] for i in range(bands)], axis=0)
+        for s in range(NY)
+    ]
+    mixed = sum(p_ref[s, 0:QROWS, :].astype(F32) * columns[s] for s in range(NY))
     for h in range(HEADS):
         flat[pl.ds(h, TOK, stride=HEADS), :] = mixed[h * TOK : (h + 1) * TOK, :]
     out[...] = flat[...].reshape(TOK, HEADS, 128).astype(BF)

time: 101 us -> 101 us (level)
  no operation moved by 1% of the time
where the time goes in v5:
time: 101 us
  starting transfers between devices  40 us (40%)
  blocking collectives  33.6 us (33%)
  Pallas kernels  18.5 us (18%)
  waiting for transfers between devices  5.16 us (5%)
  local copies, waits for them, and re-layouts  2.76 us (3%)
    ppermute x1, starting transfers between devices, on_device(): other = lax.ppermute(mine, 'zh', [(0, 1), (1, 0)])  15.4 us
    all_to_all x1, blocking collectives, on_device(): back = lax.all_to_all(out, 'y', 0, 0)  13.6 us
    all_to_all x1, blocking collectives, on_device(): along_x = lax.all_to_all(packed, 'x', 0, 0)  11.8 us
    pallas_call x1, Pallas kernels, on_device(): pl.pallas_call(attend_kernel, out_shape=jax.ShapeDtypeStruct((NY, OUTR, 1...  9.59 us
    ppermute x1, starting transfers between devices, on_device(): from_core = lax.ppermute(along_x, 'c', [(0, 1), (1, 0)])  8.48 us
    all_to_all x1, blocking collectives, on_device(): quad = lax.all_to_all(packed, 'zr', 0, 0)  8.24 us
    ppermute x1, starting transfers between devices, on_device(): other_half = lax.ppermute(half, ('zq', 'zr', 'zh'), mirrored())  6.93 us
    all_to_all x1, starting transfers between devices, on_device(): mine = jnp.sum(lax.all_to_all(partial, 'x', 0, 0), axis=0)  4.84 us
  transfers between devices with their start and end apart: 5, of which 3 were waited for; matrix products, arithmetic and copies ran while one was open for 0% of the time, Pallas kernels for 3%

profile of v5, /device:TPU:1, one launch (start us, length us, event | category | flops | bytes accessed | tf_op | source)
XLA Modules:
  0.0 100.6 jit_solution(4245184671258228012)
XLA Ops:
  0.0 0.0 copy-start.6
  0.0 0.0 copy-start.4
  0.0 2.5 %project.1 = f32[4,72,128]{2,1,0:T(8,128)} custom-call(bf16[64,896]{1,0:T(8,128)(2,1)} %hidden.1, bf16[576,896]{1,0:T(8,128)(2,1)} %bitcast.9), custom_call_target="tpu_custom_call" | custom-call | tf_op jit(solution)/shard_map/project/pallas_call | solution.py:383
  2.5 4.8 %all-to-all-start.1 = ((f32[4,72,128]{2,1,0:T(8,128)}), f32[4,72,128]{2,1,0:T(8,128)S(1)}, u32[]{:S(2)}, u32[]{:S(2)}) async-start(f32[4,72,128]{2,1,0:T(8,128)} %project.1), calls=%async_computation.1 | async-start | bytes 294912 | tf_op jit(solution)/shard_map/all_to_all | solution.py:391
  7.4 0.2 fusion
  7.6 0.1 pad_maximum_fusion
  7.7 0.0 copy-start.2
  7.7 1.1 %copy-done.2 = bf16[4,128,576]{1,2,0:T(8,128)(2,1)S(1)} copy-done((bf16[4,128,576]{1,2,0:T(8,128)(2,1)S(1)}, bf16[4,128,576]{1,2,0:T(8,128)(2,1)}, u32[]{:S(2)}) %copy-start.2) | copy-done | bytes 589848
  8.7 0.0 copy-start.3
  8.7 0.9 copy-done.3
  9.7 0.0 copy-start.5
  9.7 0.7 copy-done.5
  10.3 2.6 %prepare.1 = bf16[4,848,128]{2,1,0:T(8,128)(2,1)} custom-call(s32[2]{0:T(128)S(1)} %copy-done.5, bf16[64,8,192]{2,1,0:T(8,128)(2,1)S(1)} %copy-done.3, f32[64,64]{1,0:T(8,128)S(1)} %get-tuple-element.13.cos_ref, f32[64,64]{1,0:T(8,128)S(1)} %get-tuple-element.14.sin_ref, bf16[4,576,128]{2,1,0:T(8,128)(2,1)S(1)} %bitcast.7), custom_call_target="tpu_custom_call" | custom-call | tf_op jit(solution)/shard_map/prepare/pallas_call | solution.py:366
  12.9 0.0 copy-start
  12.9 0.0 all-to-all-done.1
  12.9 4.3 %all-to-all-start = ((bf16[4,848,128]{2,1,0:T(8,128)(2,1)}), bf16[4,848,128]{2,1,0:T(8,128)(2,1)S(1)}, u32[]{:S(2)}, u32[]{:S(2)}) async-start(bf16[4,848,128]{2,1,0:T(8,128)(2,1)} %prepare.1), calls=%async_computation | async-start | bytes 1736704 | tf_op jit(solution)/shard_map/all_to_all | solution.py:381
  17.2 0.0 copy-done.6
  17.3 15.4 %collective-permute-start = (f32[72,128]{1,0:T(8,128)S(1)}, f32[72,128]{1,0:T(8,128)S(1)}, u32[]{:S(2)}, u32[]{:S(2)}) collective-permute-start(f32[72,128]{1,0:T(8,128)S(1)} %reduce_sum.9.s_ref), channel_id=1, source_target_pairs={{0,4},{4,0},{1,5},{5,1},{2,6},{6,2},{3,7},{7,3},{8,12},{12,8},{9,1... | collective-permute-start | bytes 110600 | tf_op jit(solution)/shard_map/ppermute | solution.py:392
  32.8 0.1 concatenate.9.ids
  32.8 1.2 %collective-permute-done.r_ref = f32[72,128]{1,0:T(8,128)S(1)} collective-permute-done((f32[72,128]{1,0:T(8,128)S(1)}, f32[72,128]{1,0:T(8,128)S(1)}, u32[]{:S(2)}, u32[]{:S(2)}) %collective-permute-start) | collective-permute-done | bytes 36896 | tf_op jit(solution)/shard_map/ppermute | solution.py:392
  34.1 0.0 all-to-all-done.q_ref.p_ref
  34.1 0.0 copy-done.4
  34.1 0.7 norm.1
  34.7 8.2 %all_to_all.25.z_ref = bf16[4,144,128]{2,1,0:T(8,128)(2,1)S(1)} all-to-all(bf16[4,144,128]{2,1,0:T(8,128)(2,1)S(1)} %norm.1), channel_id=1, replica_groups=mesh['y'=4,'zq'=2,'zr'=4,'c'=2,'zh'=2,'x'=4] {'zr'}, dimensions={0} | all-to-all | bytes 294912 | tf_op jit(solution)/shard_map/all_to_all | solution.py:413
  43.0 0.6 half.1.own
  43.6 6.9 %collective-permute-start.1 = (bf16[368,128]{1,0:T(8,128)(2,1)S(1)}, bf16[368,128]{1,0:T(8,128)(2,1)S(1)}, u32[]{:S(2)}, u32[]{:S(2)}) collective-permute-start(bf16[368,128]{1,0:T(8,128)(2,1)S(1)} %half.1.own), channel_id=1, source_target_pairs={{0,116},{16,100},{32,80},{48,64},{64,48},{80,32},{96,20},{112,4},{... | collective-permute-start | bytes 282632 | tf_op jit(solution)/shard_map/ppermute | solution.py:422
  50.5 3.0 %collective-permute-done.1.other = bf16[368,128]{1,0:T(8,128)(2,1)S(1)} collective-permute-done((bf16[368,128]{1,0:T(8,128)(2,1)S(1)}, bf16[368,128]{1,0:T(8,128)(2,1)S(1)}, u32[]{:S(2)}, u32[]{:S(2)}) %collective-permute-start.1) | collective-permute-done | bytes 94240 | tf_op jit(solution)/shard_map/ppermute | solution.py:422
  53.5 0.6 pack.1
  54.1 0.0 copy-start.1
  54.1 11.8 %all_to_all.26.here = bf16[4,656,128]{2,1,0:T(8,128)(2,1)S(1)} all-to-all(bf16[4,656,128]{2,1,0:T(8,128)(2,1)S(1)} %pack.1), channel_id=1, replica_groups=mesh['y'=4,'zq'=2,'zr'=4,'c'=2,'zh'=2,'x'=4] {'x'}, dimensions={0} | all-to-all | bytes 1343488 | tf_op jit(solution)/shard_map/all_to_all | solution.py:431
  66.0 8.5 %collective-permute-start.2 = (bf16[4,656,128]{2,1,0:T(8,128)(2,1)S(1)}, bf16[4,656,128]{2,1,0:T(8,128)(2,1)S(1)}, u32[]{:S(2)}, u32[]{:S(2)}) collective-permute-start(bf16[4,656,128]{2,1,0:T(8,128)(2,1)S(1)} %all_to_all.26.here), channel_id=1, source_target_pairs={{0,8},{8,0},{1,9},{9,1},{2,10},{10,2},{3,11},{11,3},{4,12},{12,4},... | collective-permute-start | bytes 2015240 | tf_op jit(solution)/shard_map/ppermute | solution.py:432
  74.5 0.0 copy-done
  74.5 0.7 absorb.1.qfull
  75.2 1.0 collective-permute-done.2.there
  76.2 0.0 copy-done.1
  76.2 9.6 %attend.1 = bf16[4,544,128]{2,1,0:T(8,128)(2,1)S(1)} custom-call(s32[12]{0:T(128)S(1)} %concatenate.9.ids, bf16[2048,576]{1,0:T(8,128)(2,1)S(1)} %absorb.1.qfull, bf16[4,656,128]{2,1,0:T(8,128)(2,1)S(1)} %all_to_all.26.here, bf16[4,656,128]{2,1,0:T(8,128)(2,1)S(1)} %collective-permute-done.2.there, bf16[8,512,128]{2,1,0:T(8,128)(2,1)S(1)} %copy-done.1), custom_call_target="tpu_custom_call" | custom-call | tf_op jit(solution)/shard_map/attend/pallas_call | solution.py:441
  85.8 13.6 %all_to_all.27.p_ref = bf16[4,544,128]{2,1,0:T(8,128)(2,1)S(1)} all-to-all(bf16[4,544,128]{2,1,0:T(8,128)(2,1)S(1)} %attend.1), channel_id=1, replica_groups=mesh['y'=4,'zq'=2,'zr'=4,'c'=2,'zh'=2,'x'=4] {'y'}, dimensions={0} | all-to-all | bytes 1114112 | tf_op jit(solution)/shard_map/all_to_all | solution.py:453
  99.3 1.2 %merge.1 = bf16[64,8,128]{2,1,0:T(8,128)(2,1)} custom-call(bf16[4,544,128]{2,1,0:T(8,128)(2,1)S(1)} %all_to_all.27.p_ref), custom_call_target="tpu_custom_call" | custom-call | tf_op jit(solution)/shard_map/merge/pallas_call | solution.py:454
  (5 shorter events, 0.1 us)
Async XLA Ops:
  0.0 17.2 %copy-start.6 = (s32[2]{0:T(128)S(1)}, s32[2]{0:T(128)}, u32[]{:S(2)}) copy-start(s32[2]{0:T(128)} %hit.1) | copy-start | bytes 28
  0.0 34.1 %copy-start.4 = (f32[512]{0:T(512)S(1)}, f32[512]{0:T(512)}, u32[]{:S(2)}) copy-start(f32[512]{0:T(512)} %param.10) | copy-start | bytes 6148
  2.5 10.4 %all-to-all-start.1 = ((f32[4,72,128]{2,1,0:T(8,128)}), f32[4,72,128]{2,1,0:T(8,128)S(1)}, u32[]{:S(2)}, u32[]{:S(2)}) async-start(f32[4,72,128]{2,1,0:T(8,128)} %project.1), calls=%async_computation.1 | async-start | bytes 294912 | tf_op jit(solution)/shard_map/all_to_all | solution.py:391
  7.7 1.1 %copy-start.2 = (bf16[4,128,576]{1,2,0:T(8,128)(2,1)S(1)}, bf16[4,128,576]{1,2,0:T(8,128)(2,1)}, u32[]{:S(2)}) copy-start(bf16[4,128,576]{1,2,0:T(8,128)(2,1)} %param.14) | copy-start | bytes 1769476
  8.7 0.9 copy-start.3
  9.7 0.7 copy-start.5
  12.9 61.6 %copy-start = (bf16[8,128,512]{2,1,0:T(8,128)(2,1)S(1)}, bf16[8,128,512]{2,1,0:T(8,128)(2,1)}, u32[]{:S(2)}) copy-start(bf16[8,128,512]{2,1,0:T(8,128)(2,1)} %wk.1) | copy-start | bytes 3145732
  12.9 21.1 %all-to-all-start = ((bf16[4,848,128]{2,1,0:T(8,128)(2,1)}), bf16[4,848,128]{2,1,0:T(8,128)(2,1)S(1)}, u32[]{:S(2)}, u32[]{:S(2)}) async-start(bf16[4,848,128]{2,1,0:T(8,128)(2,1)} %prepare.1), calls=%async_computation | async-start | bytes 1736704 | tf_op jit(solution)/shard_map/all_to_all | solution.py:381
  17.3 16.8 %collective-permute-start = (f32[72,128]{1,0:T(8,128)S(1)}, f32[72,128]{1,0:T(8,128)S(1)}, u32[]{:S(2)}, u32[]{:S(2)}) collective-permute-start(f32[72,128]{1,0:T(8,128)S(1)} %reduce_sum.9.s_ref), channel_id=1, source_target_pairs={{0,4},{4,0},{1,5},{5,1},{2,6},{6,2},{3,7},{7,3},{8,12},{12,8},{9,1... | collective-permute-start | bytes 110600 | tf_op jit(solution)/shard_map/ppermute | solution.py:392
  43.6 9.9 %collective-permute-start.1 = (bf16[368,128]{1,0:T(8,128)(2,1)S(1)}, bf16[368,128]{1,0:T(8,128)(2,1)S(1)}, u32[]{:S(2)}, u32[]{:S(2)}) collective-permute-start(bf16[368,128]{1,0:T(8,128)(2,1)S(1)} %half.1.own), channel_id=1, source_target_pairs={{0,116},{16,100},{32,80},{48,64},{64,48},{80,32},{96,20},{112,4},{... | collective-permute-start | bytes 282632 | tf_op jit(solution)/shard_map/ppermute | solution.py:422
  54.1 22.1 %copy-start.1 = (bf16[8,512,128]{2,1,0:T(8,128)(2,1)S(1)}, bf16[8,512,128]{2,1,0:T(8,128)(2,1)}, u32[]{:S(2)}) copy-start(bf16[8,512,128]{2,1,0:T(8,128)(2,1)} %wv.1) | copy-start | bytes 3145732
  66.0 10.2 %collective-permute-start.2 = (bf16[4,656,128]{2,1,0:T(8,128)(2,1)S(1)}, bf16[4,656,128]{2,1,0:T(8,128)(2,1)S(1)}, u32[]{:S(2)}, u32[]{:S(2)}) collective-permute-start(bf16[4,656,128]{2,1,0:T(8,128)(2,1)S(1)} %all_to_all.26.here), channel_id=1, source_target_pairs={{0,8},{8,0},{1,9},{9,1},{2,10},{10,2},{3,11},{11,3},{4,12},{12,4},... | collective-permute-start | bytes 2015240 | tf_op jit(solution)/shard_map/ppermute | solution.py:432
